TPU v7x, 128 devices: a whole 4x4x4 slice. The times are simulated.
128 devices in a mesh: fsdp: 128 (over x, z, y, core).
Axes of the slice: x: 4, y: 4, z: 4, core: 2. Of those that a mesh axis runs over, the one named last changes fastest.
Arguments:
- tokens: bfloat16 [2, 16384, 1024], P(None, 'fsdp'), may hold values from -6 to 6
- cotangent: bfloat16 [2, 16384, 1024], P(None, 'fsdp'), may hold values from -6 to 6
- decays: bfloat16 [2, 16384, 24], P(None, 'fsdp'), as said below
- route: int32 [2, 16384], replicated, may hold values from 0 to 16383, as said below
- lengths: int32 [2, 128, 2], P(None, 'fsdp'), may hold values from 0 to 128, as said below
- adapter_ids: int32 [2, 128, 2], P(None, 'fsdp'), may hold values from 0 to 7
- gain_mix: float32 [1024], replicated, may hold values from 0.5 to 1.5
- gain_ffn: float32 [1024], replicated, may hold values from 0.5 to 1.5
- persistent: bfloat16 [2, 16, 1024], replicated, may hold values from -6 to 6
- w_in: bfloat16 [1024, 7168], P('fsdp'), may hold values from -0.1875 to 0.1875
- w_out: bfloat16 [1024, 1024], P('fsdp'), may hold values from -0.5 to 0.5
- w_up: bfloat16 [1024, 5632], P('fsdp'), may hold values from -0.1875 to 0.1875
- w_down: bfloat16 [2816, 1024], P('fsdp'), may hold values from -0.109375 to 0.109375
- in_down: bfloat16 [8, 1024, 112], P(None, 'fsdp'), may hold values from -0.1875 to 0.1875
- in_up: bfloat16 [8, 112, 1024], P(None, None, 'fsdp'), may hold values from -1.5 to 1.5
- out_down: bfloat16 [8, 1024, 16], P(None, 'fsdp'), may hold values from -0.1875 to 0.1875
- out_up: bfloat16 [8, 16, 1024], P(None, None, 'fsdp'), may hold values from -1.5 to 1.5
- up_down: bfloat16 [8, 1024, 32], P(None, 'fsdp'), may hold values from -0.1875 to 0.1875
- up_up: bfloat16 [8, 32, 2816], P(None, None, 'fsdp'), may hold values from -1.5 to 1.5
- down_down: bfloat16 [8, 2816, 16], P(None, 'fsdp'), may hold values from -0.109375 to 0.109375
- down_up: bfloat16 [8, 16, 1024], P(None, None, 'fsdp'), may hold values from -1.5 to 1.5
Outputs:
- activations: bfloat16 [2, 16384, 1024], P(None, 'fsdp')
- input_grad: bfloat16 [2, 16384, 1024], P(None, 'fsdp')
- grad_in_down: float32 [8, 1024, 112], P(None, 'fsdp')
- grad_in_up: float32 [8, 112, 1024], P(None, None, 'fsdp')
- grad_out_down: float32 [8, 1024, 16], P(None, 'fsdp')
- grad_out_up: float32 [8, 16, 1024], P(None, None, 'fsdp')
- grad_up_down: float32 [8, 1024, 32], P(None, 'fsdp')
- grad_up_up: float32 [8, 32, 2816], P(None, None, 'fsdp')
- grad_down_down: float32 [8, 2816, 16], P(None, 'fsdp')
- grad_down_up: float32 [8, 16, 1024], P(None, None, 'fsdp')
Inputs may be any that keep to these rules, and one draw needn't show every extreme that they name: route[m] is a permutation; of the 128 tokens in each aligned block of route's second dimension, exactly one goes to each aligned block of 128 working rows. Each group's lengths are multiples of 64 that sum to 128; zeros only after the last sequence. `decays`: retention and momentum lie in (0, 1], steps are positive.
All inputs are finite; a program needn't handle non-finite values.
Results may differ from a plain program's by a relative error of at most 0.018.
The roundings to bfloat16 on the way count: a program that leaves them out, or rounds other values in their place, can miss the bound.
Values may be sent and summed in bfloat16 or wider, within the bound.
A program may use at most 256 MiB of HBM per device.

v0:
```python
import math

import jax
import jax.numpy as jnp
from jax import lax
from jax.sharding import PartitionSpec as P

D = 1024
H = 8
HEAD = 128
R = 16
NAD = 8
NP = 16
SPAN = 64
LOCAL_BATCH_SPAN = 128
SLOTS = 2


EPS = 1e-05
HIGH = lax.Precision.HIGHEST


def plain_dot(left, right):
    return jnp.dot(left, right, preferred_element_type=jnp.float32)


def dot_right_t(left, right):
    return lax.dot_general(
        left, right, (((1,), (1,)), ((), ())), preferred_element_type=jnp.float32
    )


def dot_left_t(left, right):
    return lax.dot_general(
        left, right, (((0,), (0,)), ((), ())), preferred_element_type=jnp.float32
    )


def layout(length_row, id_row):
    seq_ends = jnp.cumsum(length_row)
    places = jnp.arange(LOCAL_BATCH_SPAN, dtype=jnp.int32)
    member = jnp.sum((seq_ends[None, :] <= places[:, None]).astype(jnp.int32), axis=1)
    slot_hit = member[:, None] == jnp.arange(SLOTS, dtype=jnp.int32)[None, :]
    chosen = jnp.sum(jnp.where(slot_hit, id_row[None, :], 0), axis=1)
    chooser = (chosen[:, None] == jnp.arange(NAD, dtype=jnp.int32)[None, :]).astype(jnp.float32)
    permitted = (member[:, None] == member[None, :]) & (places[:, None] >= places[None, :])
    before = jnp.concatenate([member[:1] - 1, member[:-1]])
    starts_new = (member != before).astype(jnp.float32)
    return (chooser, permitted, starts_new)


def norm_rows(values, gain):
    return values * lax.rsqrt(jnp.mean(values * values, axis=-1, keepdims=True) + EPS) * gain


def adapted_fwd(left, weight, down, upward, chooser, parts):
    count_rows, width_in = left.shape
    width_out = weight.shape[1] // parts
    base = plain_dot(left, weight)
    down_all = jnp.transpose(down, (1, 0, 2)).reshape(width_in, NAD * parts * R)
    latent = plain_dot(left, down_all).reshape(count_rows, NAD, parts * R) * chooser[:, :, None]
    latent = latent.astype(jnp.bfloat16).reshape(count_rows, NAD, parts, R)
    up_all = upward.reshape(NAD, parts, R, width_out)
    pieces = []
    for part_index in range(parts):
        pieces.append(
            plain_dot(
                latent[:, :, part_index, :].reshape(count_rows, NAD * R),
                up_all[:, part_index].reshape(NAD * R, width_out),
            )
        )
    return (base + jnp.concatenate(pieces, axis=1), latent)


def adapted_bwd(grad_out, left, weight, down, upward, latent, chooser, parts):
    count_rows, width_in = left.shape
    width_out = weight.shape[1] // parts
    grad_half = grad_out.astype(jnp.bfloat16)
    grad_left = dot_right_t(grad_half, weight)
    up_all = upward.reshape(NAD, parts, R, width_out)
    latent_terms = []
    upward_terms = []
    for part_index in range(parts):
        grad_part = grad_half[:, part_index * width_out : (part_index + 1) * width_out]
        up_part = up_all[:, part_index].reshape(NAD * R, width_out)
        latent_terms.append(dot_right_t(grad_part, up_part).reshape(count_rows, NAD, R))
        upward_terms.append(
            dot_left_t(latent[:, :, part_index, :].reshape(count_rows, NAD * R), grad_part).reshape(
                NAD, R, width_out
            )
        )
    grad_latent = (
        jnp.stack(latent_terms, axis=2).reshape(count_rows, NAD, parts * R) * chooser[:, :, None]
    )
    grad_latent = grad_latent.astype(jnp.bfloat16).reshape(count_rows, NAD * parts * R)
    down_all = jnp.transpose(down, (1, 0, 2)).reshape(width_in, NAD * parts * R)
    grad_left = grad_left + dot_right_t(grad_latent, down_all)
    grad_down = dot_left_t(left, grad_latent).reshape(width_in, NAD, parts * R).transpose(1, 0, 2)
    grad_upward = jnp.stack(upward_terms, axis=1).reshape(NAD, parts * R, width_out)
    return (grad_left, grad_down, grad_upward)


def attend_fwd(queries, key_rows, value_rows, persistent, permitted):
    count_rows = queries.shape[0]
    all_keys = jnp.concatenate([persistent[0], key_rows], axis=0)
    all_values = jnp.concatenate([persistent[1], value_rows], axis=0)
    q_heads = queries.reshape(count_rows, H, HEAD).transpose(1, 0, 2)
    k_heads = all_keys.reshape(NP + count_rows, H, HEAD).transpose(1, 0, 2)
    v_heads = all_values.reshape(NP + count_rows, H, HEAD).transpose(1, 0, 2)
    raw_scores = jnp.einsum("hid,hjd->hij", q_heads, k_heads, preferred_element_type=jnp.float32)
    visible = jnp.concatenate([jnp.ones((count_rows, NP), dtype=bool), permitted], axis=1)
    scaled = jnp.where(visible[None], raw_scores * (1.0 / math.sqrt(HEAD)), -1000000000.0)
    row_top = jnp.max(scaled, axis=-1, keepdims=True)
    expos = jnp.exp(scaled - row_top)
    probs = expos / jnp.sum(expos, axis=-1, keepdims=True)
    probs_half = probs.astype(jnp.bfloat16)
    result = jnp.einsum("hij,hjd->hid", probs_half, v_heads, preferred_element_type=jnp.float32)
    return (
        result.transpose(1, 0, 2).reshape(count_rows, D),
        (q_heads, k_heads, v_heads, probs, probs_half),
    )


def attend_bwd(grad_att, kept):
    q_heads, k_heads, v_heads, probs, probs_half = kept
    count_rows = q_heads.shape[1]
    grad_heads = grad_att.astype(jnp.bfloat16).reshape(count_rows, H, HEAD).transpose(1, 0, 2)
    grad_probs = jnp.einsum("hid,hjd->hij", grad_heads, v_heads, preferred_element_type=jnp.float32)
    grad_values = jnp.einsum(
        "hij,hid->hjd", probs_half, grad_heads, preferred_element_type=jnp.float32
    )
    grad_scores = (
        probs
        * (grad_probs - jnp.sum(grad_probs * probs, axis=-1, keepdims=True))
        * (1.0 / math.sqrt(HEAD))
    )
    grad_scores = grad_scores.astype(jnp.bfloat16)
    grad_queries = jnp.einsum(
        "hij,hjd->hid", grad_scores, k_heads, preferred_element_type=jnp.float32
    )
    grad_keys = jnp.einsum("hij,hid->hjd", grad_scores, q_heads, preferred_element_type=jnp.float32)

    def to_rows(values):
        return values.transpose(1, 0, 2).reshape(values.shape[1], D)

    return (to_rows(grad_queries), to_rows(grad_keys[:, NP:]), to_rows(grad_values[:, NP:]))


def unit_heads(values):
    shaped = values.reshape(values.shape[0], H, HEAD)
    return (
        shaped
        * lax.rsqrt(jnp.mean(shaped * shaped, axis=-1, keepdims=True) + EPS)
        * (1.0 / math.sqrt(HEAD))
    )


def remember(mem_keys, mem_values, mem_queries, decay_rows, starts_new):
    count_rows = mem_keys.shape[0]
    blocks = count_rows // SPAN

    def by_block(values):
        return values.reshape(blocks, SPAN, H, HEAD).transpose(0, 2, 1, 3)

    def by_rate(values):
        return values.reshape(blocks, SPAN, H).transpose(0, 2, 1)

    key_blocks = by_block(unit_heads(mem_keys))
    query_blocks = by_block(unit_heads(mem_queries))
    value_blocks = by_block(mem_values)
    log_retain = by_rate(jnp.log(decay_rows[:, :H]))
    log_moment = by_rate(jnp.log(decay_rows[:, H : 2 * H]))
    step_sizes = by_rate(decay_rows[:, 2 * H :])
    lower = jnp.arange(SPAN)[:, None] >= jnp.arange(SPAN)[None, :]
    memory = jnp.zeros((H, HEAD, HEAD), jnp.float32)
    moment = jnp.zeros((H, HEAD, HEAD), jnp.float32)
    outputs = []
    for block in range(blocks):
        keep_state = 1.0 - starts_new[block * SPAN]
        memory = memory * keep_state
        moment = moment * keep_state
        cum_retain = jnp.cumsum(log_retain[block], axis=-1)
        cum_moment = jnp.cumsum(log_moment[block], axis=-1)
        retain_pairs = jnp.exp(
            jnp.where(lower[None], cum_retain[:, :, None] - cum_retain[:, None, :], -1e30)
        )
        moment_pairs = jnp.exp(
            jnp.where(lower[None], cum_moment[:, :, None] - cum_moment[:, None, :], -1e30)
        )
        weight_pairs = jnp.einsum("hij,hjm->him", retain_pairs, moment_pairs, precision=HIGH)
        retain_run = jnp.exp(cum_retain)
        moment_run = jnp.exp(cum_moment)
        carry_run = jnp.einsum("hij,hj->hi", retain_pairs, moment_run, precision=HIGH)
        keys_now = key_blocks[block]
        queries_now = query_blocks[block]
        rates_now = step_sizes[block]
        error_terms = (
            jnp.einsum("hcp,hpq->hcq", keys_now, memory, precision=HIGH) - value_blocks[block]
        )
        affinity = (
            jnp.einsum("hip,hmp->him", queries_now, keys_now, precision=HIGH)
            * weight_pairs
            * rates_now[:, None, :]
        )
        read_now = retain_run[:, :, None] * jnp.einsum(
            "hip,hpq->hiq", queries_now, memory, precision=HIGH
        )
        read_now = read_now + carry_run[:, :, None] * jnp.einsum(
            "hip,hpq->hiq", queries_now, moment, precision=HIGH
        )
        read_now = read_now - jnp.einsum("him,hmq->hiq", affinity, error_terms, precision=HIGH)
        last_weight = weight_pairs[:, -1, :] * rates_now
        last_moment = moment_pairs[:, -1, :] * rates_now
        new_memory = retain_run[:, -1, None, None] * memory + carry_run[:, -1, None, None] * moment
        new_memory = new_memory - jnp.einsum(
            "hmp,hmq->hpq", keys_now * last_weight[:, :, None], error_terms, precision=HIGH
        )
        moment = moment_run[:, -1, None, None] * moment - jnp.einsum(
            "hmp,hmq->hpq", keys_now * last_moment[:, :, None], error_terms, precision=HIGH
        )
        memory = new_memory
        outputs.append(read_now)
    return jnp.stack(outputs).transpose(0, 2, 1, 3).reshape(count_rows, D)


def layer_both(x_rows, d_rows, adapters, frozen_set, decay_rows, chooser, permitted, starts_new):
    in_down, in_up, out_down, out_up, up_down, up_up, down_down, down_up = adapters
    gain_mix, gain_ffn, persistent, w_in, w_out, w_up, w_down = frozen_set
    h_float, pull_mix = jax.vjp(lambda values: norm_rows(values, gain_mix), x_rows)
    h_mix = h_float.astype(jnp.bfloat16)
    projected, latent_in = adapted_fwd(h_mix, w_in, in_down, in_up, chooser, 7)
    pieces = jnp.split(projected, 7, axis=1)
    attended, att_kept = attend_fwd(
        pieces[0].astype(jnp.bfloat16),
        pieces[1].astype(jnp.bfloat16),
        pieces[2].astype(jnp.bfloat16),
        persistent,
        permitted,
    )
    recalled, pull_memory = jax.vjp(
        lambda first, second, third: remember(first, second, third, decay_rows, starts_new),
        pieces[3],
        pieces[4],
        pieces[5],
    )
    opening = jax.nn.sigmoid(pieces[6])
    joined = (attended + opening * recalled).astype(jnp.bfloat16)
    branch_out, latent_out = adapted_fwd(joined, w_out, out_down, out_up, chooser, 1)
    mid_rows = x_rows + branch_out
    h2_float, pull_ffn = jax.vjp(lambda values: norm_rows(values, gain_ffn), mid_rows)
    h_ffn = h2_float.astype(jnp.bfloat16)
    gate_up, latent_up = adapted_fwd(h_ffn, w_up, up_down, up_up, chooser, 2)
    gate_part, up_part = jnp.split(gate_up, 2, axis=1)
    gate_sig = jax.nn.sigmoid(gate_part)
    gate_silu = gate_part * gate_sig
    active = (gate_silu * up_part).astype(jnp.bfloat16)
    final_out, latent_down = adapted_fwd(active, w_down, down_down, down_up, chooser, 1)
    result = mid_rows + final_out
    grad_mid = d_rows
    grad_active, grad_dd, grad_du = adapted_bwd(
        d_rows, active, w_down, down_down, down_up, latent_down, chooser, 1
    )
    silu_slope = gate_sig * (1.0 + gate_part * (1.0 - gate_sig))
    grad_gate_up = jnp.concatenate(
        [grad_active * up_part * silu_slope, grad_active * gate_silu], axis=1
    )
    grad_h_ffn, grad_ud, grad_uu = adapted_bwd(
        grad_gate_up, h_ffn, w_up, up_down, up_up, latent_up, chooser, 2
    )
    grad_mid = grad_mid + pull_ffn(grad_h_ffn)[0]
    grad_joined, grad_od, grad_ou = adapted_bwd(
        grad_mid, joined, w_out, out_down, out_up, latent_out, chooser, 1
    )
    grad_joined = grad_joined.astype(jnp.bfloat16).astype(jnp.float32)
    grad_recalled = grad_joined * opening
    grad_opening = grad_joined * recalled * opening * (1.0 - opening)
    grad_q, grad_k, grad_v = attend_bwd(grad_joined, att_kept)
    grad_mk, grad_mv, grad_mq = pull_memory(grad_recalled)
    grad_projected = jnp.concatenate(
        [grad_q, grad_k, grad_v, grad_mk, grad_mv, grad_mq, grad_opening], axis=1
    )
    grad_h_mix, grad_id, grad_iu = adapted_bwd(
        grad_projected, h_mix, w_in, in_down, in_up, latent_in, chooser, 7
    )
    grad_x = grad_mid + pull_mix(grad_h_mix)[0]
    return (
        result,
        grad_x,
        (grad_id, grad_iu, grad_od, grad_ou, grad_ud, grad_uu, grad_dd, grad_du),
    )


def body(
    tokens,
    cotangent,
    decays,
    route,
    lengths,
    adapter_ids,
    gain_mix,
    gain_ffn,
    persistent,
    w_in,
    w_out,
    w_up,
    w_down,
    in_down,
    in_up,
    out_down,
    out_up,
    up_down,
    up_up,
    down_down,
    down_up,
):
    position = lax.axis_index("fsdp")
    totals = None
    outputs = []
    gradients = []
    for micro_step in range(tokens.shape[0]):
        gathered = (
            lax.all_gather(w_in, "fsdp", axis=0, tiled=True),
            lax.all_gather(w_out, "fsdp", axis=0, tiled=True),
            lax.all_gather(w_up, "fsdp", axis=0, tiled=True),
            lax.all_gather(w_down, "fsdp", axis=0, tiled=True),
            lax.all_gather(in_down, "fsdp", axis=1, tiled=True),
            lax.all_gather(in_up, "fsdp", axis=2, tiled=True),
            lax.all_gather(out_down, "fsdp", axis=1, tiled=True),
            lax.all_gather(out_up, "fsdp", axis=2, tiled=True),
            lax.all_gather(up_down, "fsdp", axis=1, tiled=True),
            lax.all_gather(up_up, "fsdp", axis=2, tiled=True),
            lax.all_gather(down_down, "fsdp", axis=1, tiled=True),
            lax.all_gather(down_up, "fsdp", axis=2, tiled=True),
        )
        frozen_set = (
            gain_mix,
            gain_ffn,
            persistent,
            gathered[0],
            gathered[1],
            gathered[2],
            gathered[3],
        )
        adapters = tuple(gathered[4:])
        routes_all = route[micro_step]
        own_routes = lax.dynamic_slice_in_dim(
            routes_all, position * LOCAL_BATCH_SPAN, LOCAL_BATCH_SPAN
        )
        send_order = jnp.argsort(own_routes)
        sources = (
            lax.dynamic_slice_in_dim(
                jnp.argsort(routes_all), position * LOCAL_BATCH_SPAN, LOCAL_BATCH_SPAN
            )
            // LOCAL_BATCH_SPAN
        )
        arrival = jnp.argsort(
            sources * LOCAL_BATCH_SPAN + jnp.arange(LOCAL_BATCH_SPAN, dtype=jnp.int32)
        )
        placing = jnp.argsort(arrival)
        got_tokens, got_cotangent, got_decays = (
            lax.all_to_all(
                tokens[micro_step][send_order], "fsdp", split_axis=0, concat_axis=0, tiled=True
            ),
            lax.all_to_all(
                cotangent[micro_step][send_order], "fsdp", split_axis=0, concat_axis=0, tiled=True
            ),
            lax.all_to_all(
                decays[micro_step][send_order], "fsdp", split_axis=0, concat_axis=0, tiled=True
            ),
        )
        x_rows = got_tokens[placing].astype(jnp.float32)
        d_rows = got_cotangent[placing].astype(jnp.float32)
        decay_rows = got_decays[placing].astype(jnp.float32)
        chooser, permitted, starts_new = layout(lengths[micro_step, 0], adapter_ids[micro_step, 0])
        result, x_grad, adapter_grad = layer_both(
            x_rows, d_rows, adapters, frozen_set, decay_rows, chooser, permitted, starts_new
        )
        if totals is None:
            totals = adapter_grad
        else:
            totals = tuple((left + right for left, right in zip(totals, adapter_grad)))
        back_out, back_grad = (
            lax.all_to_all(
                result.astype(jnp.bfloat16)[arrival],
                "fsdp",
                split_axis=0,
                concat_axis=0,
                tiled=True,
            ),
            lax.all_to_all(
                x_grad.astype(jnp.bfloat16)[arrival],
                "fsdp",
                split_axis=0,
                concat_axis=0,
                tiled=True,
            ),
        )
        undoing = jnp.argsort(send_order)
        outputs.append(back_out[undoing])
        gradients.append(back_grad[undoing])
    summed = (
        lax.psum_scatter(totals[0], "fsdp", scatter_dimension=1, tiled=True),
        lax.psum_scatter(totals[1], "fsdp", scatter_dimension=2, tiled=True),
        lax.psum_scatter(totals[2], "fsdp", scatter_dimension=1, tiled=True),
        lax.psum_scatter(totals[3], "fsdp", scatter_dimension=2, tiled=True),
        lax.psum_scatter(totals[4], "fsdp", scatter_dimension=1, tiled=True),
        lax.psum_scatter(totals[5], "fsdp", scatter_dimension=2, tiled=True),
        lax.psum_scatter(totals[6], "fsdp", scatter_dimension=1, tiled=True),
        lax.psum_scatter(totals[7], "fsdp", scatter_dimension=2, tiled=True),
    )
    return (
        jnp.stack(outputs),
        jnp.stack(gradients),
        summed[0],
        summed[1],
        summed[2],
        summed[3],
        summed[4],
        summed[5],
        summed[6],
        summed[7],
    )


def solution(mesh):
    return jax.shard_map(
        body,
        mesh=mesh,
        in_specs=(
            P(None, "fsdp", None),
            P(None, "fsdp", None),
            P(None, "fsdp", None),
            P(),
            P(None, "fsdp", None),
            P(None, "fsdp", None),
            P(),
            P(),
            P(),
            P("fsdp", None),
            P("fsdp", None),
            P("fsdp", None),
            P("fsdp", None),
            P(None, "fsdp", None),
            P(None, None, "fsdp"),
            P(None, "fsdp", None),
            P(None, None, "fsdp"),
            P(None, "fsdp", None),
            P(None, None, "fsdp"),
            P(None, "fsdp", None),
            P(None, None, "fsdp"),
        ),
        out_specs=(
            P(None, "fsdp", None),
            P(None, "fsdp", None),
            P(None, "fsdp", None),
            P(None, None, "fsdp"),
            P(None, "fsdp", None),
            P(None, None, "fsdp"),
            P(None, "fsdp", None),
            P(None, None, "fsdp"),
            P(None, "fsdp", None),
            P(None, None, "fsdp"),
        ),
        check_vma=False,
    )
```

profile of v0, /device:TPU:1, one launch (start us, length us, event | category | flops | bytes accessed | tf_op | source)
XLA Modules:
  0.0 5348.3 jit_solution(1573841991784221973)
XLA Ops:
  18.9 11.5 all-to-all-start.4
  32.5 43.4 all_gather.52
  107.0 40.1 all_gather.53
  148.3 38.8 all_gather.55
  187.1 36.6 all_gather.59
  223.9 42.0 all_gather.58
  341.6 10.4 all-to-all-start
  353.3 12.1 all-to-all-done
  445.9 9.8 reshape.1296
  455.7 10.3 fusion.597
  481.9 10.4 fusion.601
  781.6 8.0 copy.921
  801.9 10.2 all-to-all-start.5
  813.2 10.9 fusion.608
  830.5 10.2 fusion.607
  844.1 9.9 all-to-all-start.2
  857.0 8.1 all-to-all-done.2
  901.9 582.9 %reduce-scatter.13.cloned.1.call-done = f32[8,8,16]{2,0,1:T(8,128)} async-done(((f32[8,1024,16]{2,0,1:T(8,128)}), f32[8,8,16]{2,0,1:T(8,128)}) %reduce-scatter.13.cloned.1.call-update) | async-done | bytes 4112 | tf_op jit(solution)/shard_map/reduce_scatter | solution.py:404
  1486.2 639.0 %reduce-scatter.17.cloned.1.call-done = f32[8,8,32]{2,0,1:T(8,128)} async-done(((f32[8,1024,32]{2,0,1:T(8,128)}), f32[8,8,32]{2,0,1:T(8,128)}) %reduce-scatter.17.cloned.1.call-update) | async-done | bytes 8208 | tf_op jit(solution)/shard_map/reduce_scatter | solution.py:406
  2126.5 639.0 %reduce-scatter.9.cloned.1.call-done = f32[8,8,112]{2,0,1:T(8,128)} async-done(((f32[8,1024,112]{2,0,1:T(8,128)}), f32[8,8,112]{2,0,1:T(8,128)}) %reduce-scatter.9.cloned.1.call-update) | async-done | bytes 28688 | tf_op jit(solution)/shard_map/reduce_scatter | solution.py:402
  2766.9 639.0 %reduce-scatter.11.cloned.1.call-done = f32[8,112,8]{1,0,2:T(8,128)} async-done(((f32[8,112,1024]{1,0,2:T(8,128)}), f32[8,112,8]{1,0,2:T(8,128)}) %reduce-scatter.11.cloned.1.call-update) | async-done | bytes 28688 | tf_op jit(solution)/shard_map/reduce_scatter | solution.py:403
  3407.2 639.6 %reduce-scatter.15.cloned.1.call-done = f32[8,16,8]{1,2,0:T(8,128)} async-done(((f32[8,16,1024]{1,2,0:T(8,128)}), f32[8,16,8]{1,2,0:T(8,128)}) %reduce-scatter.15.cloned.1.call-update) | async-done | bytes 4112 | tf_op jit(solution)/shard_map/reduce_scatter | solution.py:405
  4046.8 640.9 %reduce-scatter.21.cloned.1.call-done = f32[8,16,8]{1,2,0:T(8,128)} async-done(((f32[8,16,1024]{1,2,0:T(8,128)}), f32[8,16,8]{1,2,0:T(8,128)}) %reduce-scatter.21.cloned.1.call-update) | async-done | bytes 4112 | tf_op jit(solution)/shard_map/reduce_scatter | solution.py:409
  4687.7 653.7 %reduce-scatter.19.cloned.1.call-done = f32[8,32,22]{1,0,2:T(8,128)} async-done(((f32[8,32,2816]{1,0,2:T(8,128)}), f32[8,32,22]{1,0,2:T(8,128)}) %reduce-scatter.19.cloned.1.call-update) | async-done | bytes 22544 | tf_op jit(solution)/shard_map/reduce_scatter | solution.py:407
  (1284 shorter events, 569.5 us)
Async XLA Ops:
  7.2 411.3 %all-gather.19.cloned.1.call-start = ((), (), s32[]{:S(2)}) async-start(), calls=%async_computation.22 | async-start | bytes 5812224 | tf_op jit(solution)/shard_map/all_gather | solution.py:331
  8.0 417.9 %all-gather.13.cloned.1.call-start = ((), (), s32[]{:S(2)}) async-start(), calls=%async_computation.19 | async-start | bytes 2113536 | tf_op jit(solution)/shard_map/all_gather | solution.py:327
  9.3 420.6 %all-gather.11.cloned.1.call-start = ((), (), s32[]{:S(2)}) async-start(), calls=%async_computation.18 | async-start | bytes 2113536 | tf_op jit(solution)/shard_map/all_gather | solution.py:326
  10.7 435.2 %all-gather.21.cloned.1.call-start = ((), (), s32[]{:S(2)}) async-start(), calls=%async_computation.30 | async-start | bytes 6340608 | tf_op jit(solution)/shard_map/all_gather | solution.py:325
  11.3 444.4 %all-gather.9.cloned.1.call-start = ((), (), s32[]{:S(2)}) async-start(), calls=%async_computation.17 | async-start | bytes 14794752 | tf_op jit(solution)/shard_map/all_gather | solution.py:322
  11.9 505.1 %all-gather.15.cloned.1.call-start = ((), (), s32[]{:S(2)}) async-start(), calls=%async_computation.20 | async-start | bytes 2113536 | tf_op jit(solution)/shard_map/all_gather | solution.py:323
  18.9 278.5 %all-to-all-start.4 = ((bf16[128,1,24]{2,1,0:T(2,128)(2,1)}), bf16[128,1,24]{2,1,0:T(2,128)(2,1)S(1)}, u32[]{:S(2)}, u32[]{:S(2)}) async-start(bf16[128,1,24]{2,1,0:T(2,128)(2,1)} %copy.830), calls=%async_computation.4 | async-start | bytes 131072 | tf_op jit(solution)/shard_map/all_to_all | solution.py:367
  30.4 498.0 %all-gather.17.cloned.1.call-start = ((), (), s32[]{:S(2)}) async-start(), calls=%async_computation.21 | async-start | bytes 11624448 | tf_op jit(solution)/shard_map/all_gather | solution.py:324
  312.2 29.3 all-to-all-start.3
  341.6 23.9 all-to-all-start
  365.4 16.3 all-to-all-start.8
  381.7 24.5 all-to-all-start.6
  386.9 513.4 %all-reduce.17.cloned.1.call-start = ((), (), s32[]{:S(2)}) async-start(), calls=%async_computation.31 | async-start | bytes 2883584
  695.1 789.8 %reduce-scatter.13.cloned.1.call-start = ((), (), s32[]{:S(2)}) async-start(), calls=%async_computation.25 | async-start | bytes 4227072 | tf_op jit(solution)/shard_map/reduce_scatter | solution.py:404
  707.4 1417.7 %reduce-scatter.17.cloned.1.call-start = ((), (), s32[]{:S(2)}) async-start(), calls=%async_computation.27 | async-start | bytes 4227072 | tf_op jit(solution)/shard_map/reduce_scatter | solution.py:406
  722.9 2042.6 %reduce-scatter.9.cloned.1.call-start = ((), (), s32[]{:S(2)}) async-start(), calls=%async_computation.23 | async-start | bytes 4227072 | tf_op jit(solution)/shard_map/reduce_scatter | solution.py:402
  742.7 2663.2 %reduce-scatter.11.cloned.1.call-start = ((), (), s32[]{:S(2)}) async-start(), calls=%async_computation.24 | async-start | bytes 4227072 | tf_op jit(solution)/shard_map/reduce_scatter | solution.py:403
  755.7 3291.1 %reduce-scatter.15.cloned.1.call-start = ((), (), s32[]{:S(2)}) async-start(), calls=%async_computation.26 | async-start | bytes 4227072 | tf_op jit(solution)/shard_map/reduce_scatter | solution.py:405
  769.8 3917.9 %reduce-scatter.21.cloned.1.call-start = ((), (), s32[]{:S(2)}) async-start(), calls=%async_computation.29 | async-start | bytes 4227072 | tf_op jit(solution)/shard_map/reduce_scatter | solution.py:409
  776.6 4564.8 %reduce-scatter.19.cloned.1.call-start = ((), (), s32[]{:S(2)}) async-start(), calls=%async_computation.28 | async-start | bytes 11624448 | tf_op jit(solution)/shard_map/reduce_scatter | solution.py:407
  801.9 42.2 all-to-all-start.5
  844.1 21.0 all-to-all-start.2
  865.1 15.6 all-to-all-start.9
  880.7 15.9 all-to-all-start.7
  (339 other events, 3848.7 us)
Sparse Core Ops, SparseCore 0:
  11.0 72.4 all-gather.18
  86.7 65.1 all-gather.12
  155.0 62.5 all-gather.10
  220.6 66.4 all-gather.20
  289.8 80.0 all-gather.8
  372.9 65.1 all-gather.14
  441.1 69.7 all-gather.16
  695.2 150.4 all-reduce.16
  848.0 636.7 reduce-scatter.12
  1487.1 637.9 reduce-scatter.16
  2127.5 637.9 reduce-scatter.8
  2767.8 637.9 reduce-scatter.10
  3408.8 637.9 reduce-scatter.14
  4049.7 637.9 reduce-scatter.20
  4690.5 650.8 reduce-scatter.18
where the time goes:
time: 5370 us; the launch traced here: 5350 us
  waiting for transfers between devices  4490 us (84%)
  matrix products  251 us (5%)
  local copies, waits for them, and re-layouts  211 us (4%)
  blocking collectives  201 us (4%)
  other arithmetic  103 us (2%)
  starting transfers between devices  74.3 us (1%)
    reduce_scatter x1, waiting for transfers between devices, body(): lax.psum_scatter(totals[5], 'fsdp', scatter_dimension=2, tiled=True)  654 us
    reduce_scatter x1, waiting for transfers between devices, body(): lax.psum_scatter(totals[7], 'fsdp', scatter_dimension=2, tiled=True)  641 us
    reduce_scatter x1, waiting for transfers between devices, body(): lax.psum_scatter(totals[3], 'fsdp', scatter_dimension=2, tiled=True)  640 us
    reduce_scatter x1, waiting for transfers between devices, body(): lax.psum_scatter(totals[0], 'fsdp', scatter_dimension=1, tiled=True)  639 us
    reduce_scatter x1, waiting for transfers between devices, body(): lax.psum_scatter(totals[1], 'fsdp', scatter_dimension=2, tiled=True)  639 us
    reduce_scatter x1, waiting for transfers between devices, body(): lax.psum_scatter(totals[4], 'fsdp', scatter_dimension=1, tiled=True)  639 us
    reduce_scatter x1, waiting for transfers between devices, body(): lax.psum_scatter(totals[2], 'fsdp', scatter_dimension=1, tiled=True)  583 us
  transfers between devices with their start and end apart: 25, of which 13 were waited for; matrix products, arithmetic and copies ran while one was open for 7% of the time, Pallas kernels for 0%

commit v1 on v0

v1 whole, which is shorter than its diff:
```python
import functools
import math

import jax
import jax.numpy as jnp
from jax import lax
from jax.experimental import pallas as pl
from jax.experimental.pallas import tpu as pltpu
from jax.sharding import PartitionSpec as P

D = 1024
H = 8
HEAD = 128
FF = 2816
R = 16
NAD = 8
NP = 16
SPAN = 64
GROUP = 128
MB = 2
ROWS = MB * GROUP
N_DEV = 128
AR = NAD * R
HCOLS = 7 * HEAD
FF_SHARD = FF // N_DEV
FF_PAD = 24
FFP = FF_PAD * N_DEV
FB = 768
EPS = 1e-05
SCALE = 1.0 / math.sqrt(HEAD)
VMEM_LIMIT = 60 * 1024 * 1024
BF = jnp.bfloat16
F32 = jnp.float32

NN = (((1,), (0,)), ((), ()))
NT = (((1,), (1,)), ((), ()))
TN = (((0,), (0,)), ((), ()))


def dot(left, right, dims=NN):
    return lax.dot_general(left, right, dims, preferred_element_type=F32)


def exact(left, right, dims=NN):
    return lax.dot_general(
        left, right, dims, precision=lax.Precision.HIGHEST, preferred_element_type=F32
    )


def halves(value):
    high = value.astype(BF)
    return high, (value - high.astype(F32)).astype(BF)


def dot3(left, right, dims=NN):
    lh, ll = left
    rh, rl = right
    return dot(lh, rh, dims) + (dot(lh, rl, dims) + dot(ll, rh, dims))


def norm_fwd(values, gain):
    inv = lax.rsqrt(jnp.mean(values * values, axis=-1, keepdims=True) + EPS)
    return values * inv * gain, inv


def norm_bwd(grad, values, inv, gain):
    scaled = grad * gain
    return inv * (scaled - values * (inv * inv * jnp.mean(values * scaled, axis=-1, keepdims=True)))


def decay_kernel(keep_ref, dec_ref, dect_ref, wf_ref, lw_ref):
    rows = lax.broadcasted_iota(jnp.int32, (GROUP, GROUP), 0)
    cols = lax.broadcasted_iota(jnp.int32, (GROUP, GROUP), 1)
    lower = (rows >= cols) & ((rows >= SPAN) == (cols >= SPAN))
    tri = lower.astype(F32)
    second = rows >= SPAN
    for g in range(MB):
        keep = keep_ref[g]
        here = dec_ref[g * GROUP : (g + 1) * GROUP, :]
        here_t = dect_ref[:, g * GROUP : (g + 1) * GROUP]
        run = exact(tri, jnp.log(here[:, : 2 * H]))
        run_t = exact(jnp.log(here_t[: 2 * H, :]), tri, NT)
        for h in range(H):
            gap = run[:, h : h + 1] - run_t[h : h + 1, :]
            retain = jnp.exp(jnp.where(lower, gap, -1e30))
            gap = run[:, H + h : H + h + 1] - run_t[H + h : H + h + 1, :]
            moment = jnp.exp(jnp.where(lower, gap, -1e30))
            pairs = exact(retain, moment)
            theta = here_t[2 * H + h : 2 * H + h + 1, :]
            moment_run = jnp.exp(run_t[H + h : H + h + 1, :])
            carry = jnp.sum(retain * moment_run, axis=1, keepdims=True)
            last_weight = pairs[SPAN - 1 : SPAN, :] * theta * keep
            last_moment = moment[SPAN - 1 : SPAN, :] * theta * keep
            across = jnp.exp(run[:, h : h + 1]) * last_weight + carry * last_moment
            wf_ref[h, g] = pairs * theta + jnp.where(second, across, 0.0)
            lw_ref[h, g] = jnp.broadcast_to(last_weight, (8, GROUP))


def decay_weights(keep, dec, dec_t):
    return pl.pallas_call(
        decay_kernel,
        out_shape=(
            jax.ShapeDtypeStruct((H, MB, GROUP, GROUP), F32),
            jax.ShapeDtypeStruct((H, MB, 8, GROUP), F32),
        ),
        in_specs=[
            pl.BlockSpec(memory_space=pltpu.SMEM),
            pl.BlockSpec(memory_space=pltpu.VMEM),
            pl.BlockSpec(memory_space=pltpu.VMEM),
        ],
        out_specs=(
            pl.BlockSpec(memory_space=pltpu.VMEM),
            pl.BlockSpec(memory_space=pltpu.VMEM),
        ),
        name="decays",
    )(keep, dec, dec_t)


def allowed_mask(split_ref):
    rows = lax.broadcasted_iota(jnp.int32, (ROWS, GROUP), 0)
    cols = lax.broadcasted_iota(jnp.int32, (ROWS, GROUP), 1)
    local = rows % GROUP
    group = rows // GROUP
    split = jnp.where(group == 0, split_ref[0], split_ref[1]) > 0.5
    return (local >= cols) & jnp.logical_not(split & (local >= SPAN) & (cols < SPAN))


def by_group(make):
    return jnp.concatenate([make(slice(0, GROUP), 0), make(slice(GROUP, ROWS), 1)], axis=0)


def attend(q, k, v, pk, pv, allowed):
    near = by_group(lambda s, g: dot(q[s], k[s], NT))
    far = dot(q, pk, NT) * SCALE
    near = jnp.where(allowed, near * SCALE, -1000000000.0)
    top = jnp.maximum(
        jnp.max(near, axis=-1, keepdims=True), jnp.max(far, axis=-1, keepdims=True)
    )
    near = jnp.exp(near - top)
    far = jnp.exp(far - top)
    inv = 1.0 / (jnp.sum(near, axis=-1, keepdims=True) + jnp.sum(far, axis=-1, keepdims=True))
    near = near * inv
    far = far * inv
    return near, far


def attend_out(near_half, far_half, v, pv):
    return by_group(lambda s, g: dot(near_half[s], v[s])) + dot(far_half, pv)


def unit(values):
    inv = lax.rsqrt(jnp.mean(values * values, axis=-1, keepdims=True) + EPS)
    return values * (inv * SCALE), inv


def unit_bwd(grad, values, inv):
    return (inv * SCALE) * (
        grad - values * (inv * inv * jnp.mean(values * grad, axis=-1, keepdims=True))
    )


def memory_terms(kn, qn, mv, wf_ref, lw_ref):
    second = lax.broadcasted_iota(jnp.int32, (GROUP, GROUP), 0) >= SPAN
    kept = []
    for g in range(MB):
        s = slice(g * GROUP, (g + 1) * GROUP)
        kh, qh = halves(kn[s]), halves(qn[s])
        wf = wf_ref[0, g]
        lw = jnp.where(second, lw_ref[0, g][0:1, :], 0.0)
        kk = dot3(kh, kh, NT) * lw
        qk = dot3(qh, kh, NT) * wf
        kk_half = halves(kk)
        mvh = halves(mv[s])
        err = mv[s] - dot3(kk_half, mvh)
        errh = halves(err)
        qk_half = halves(qk)
        kept.append((kh, qh, wf, lw, kk_half, qk_half, mvh, errh))
    return kept


def memory_out(kept):
    return jnp.concatenate([dot3(item[5], item[7]) for item in kept], axis=0)


def memory_bwd(kept, grad):
    grads_k, grads_q, grads_v = [], [], []
    for g in range(MB):
        kh, qh, wf, lw, kk_half, qk_half, mvh, errh = kept[g]
        gh = halves(grad[g * GROUP : (g + 1) * GROUP])
        d_qk = dot3(gh, errh, NT) * wf
        d_err = dot3(qk_half, gh, TN)
        deh = halves(d_err)
        d_v = d_err - dot3(kk_half, deh, TN)
        d_kk = dot3(deh, mvh, NT) * lw
        dqh = halves(d_qk)
        dkh = halves(d_kk)
        grads_q.append(dot3(dqh, kh))
        grads_k.append(dot3(dqh, qh, TN) - (dot3(dkh, kh) + dot3(dkh, kh, TN)))
        grads_v.append(d_v)
    return (
        jnp.concatenate(grads_k, axis=0),
        jnp.concatenate(grads_q, axis=0),
        jnp.concatenate(grads_v, axis=0),
    )


def heads_fwd_kernel(
    split_ref, x_ref, gain_ref, mask_ref, w_ref, down_ref, up_ref, pers_ref, wf_ref, lw_ref,
    proj_ref, z_ref, h1_ref, lat_ref,
):
    @pl.when(pl.program_id(0) == 0)
    def _():
        normed, _ = norm_fwd(x_ref[...].astype(F32), gain_ref[...])
        h1_ref[...] = normed.astype(BF)
        latent = dot(h1_ref[...], down_ref[0])
        mask = mask_ref[...]
        for part in range(7):
            s = slice(part * AR, (part + 1) * AR)
            lat_ref[:, s] = (latent[:, s] * mask).astype(BF)

    base = dot(h1_ref[...], w_ref[0])
    pieces = []
    for part in range(7):
        s = slice(part * AR, (part + 1) * AR)
        piece = base[:, part * HEAD : (part + 1) * HEAD] + dot(lat_ref[:, s], up_ref[0, :, s], NT)
        proj_ref[:, part * HEAD : (part + 1) * HEAD] = piece
        pieces.append(piece)
    q, k, v = (pieces[i].astype(BF) for i in range(3))
    near, far = attend(q, k, v, pers_ref[0], pers_ref[1], allowed_mask(split_ref))
    att = attend_out(near.astype(BF), far.astype(BF), v, pers_ref[1])
    kn, _ = unit(pieces[3])
    qn, _ = unit(pieces[5])
    mem = memory_out(memory_terms(kn, qn, pieces[4], wf_ref, lw_ref))
    z_ref[...] = (att + jax.nn.sigmoid(pieces[6]) * mem).astype(BF)


def heads_fwd(split, x, gain, mask, a1, persistent, wf, lw):
    return pl.pallas_call(
        heads_fwd_kernel,
        grid=(H,),
        out_shape=(
            jax.ShapeDtypeStruct((ROWS, 7 * D), F32),
            jax.ShapeDtypeStruct((ROWS, D), BF),
            jax.ShapeDtypeStruct((ROWS, D), BF),
            jax.ShapeDtypeStruct((ROWS, 7 * AR), BF),
        ),
        in_specs=[
            pl.BlockSpec(memory_space=pltpu.SMEM),
            pl.BlockSpec((ROWS, D), lambda h: (0, 0)),
            pl.BlockSpec((1, D), lambda h: (0, 0)),
            pl.BlockSpec((ROWS, AR), lambda h: (0, 0)),
            pl.BlockSpec((1, D, HCOLS), lambda h: (h // 4, 0, h % 4)),
            pl.BlockSpec((1, D, HCOLS), lambda h: (0, 0, 4)),
            pl.BlockSpec((1, HEAD, HCOLS), lambda h: (1, h, 4)),
            pl.BlockSpec((2, NP, HEAD), lambda h: (0, 0, h)),
            pl.BlockSpec((1, MB, GROUP, GROUP), lambda h: (h, 0, 0, 0)),
            pl.BlockSpec((1, MB, 8, GROUP), lambda h: (h, 0, 0, 0)),
        ],
        out_specs=(
            pl.BlockSpec((ROWS, HCOLS), lambda h: (0, h)),
            pl.BlockSpec((ROWS, HEAD), lambda h: (0, h)),
            pl.BlockSpec((ROWS, D), lambda h: (0, 0)),
            pl.BlockSpec((ROWS, 7 * AR), lambda h: (0, 0)),
        ),
        compiler_params=pltpu.CompilerParams(vmem_limit_bytes=VMEM_LIMIT),
        name="heads_fwd",
    )(split, x, gain, mask, a1, a1, a1, persistent, wf, lw)


def ffn_kernel(
    x_ref, d_ref, z_ref, gain_ref, mask_ref, place_ref, w_out_ref, small_ref, w_up_ref, wd0_ref, wd1_ref,
    back_ref, dz_ref, dmid_ref, grads_ref,
    x2_ref, h2_ref, inv_ref, lat_out_ref, lat_up_ref, dl_down_ref, acc_ref, lat_acc_ref, dh_ref, dlat_ref,
):
    step = pl.program_id(0)
    out_down = lambda: small_ref[0, :, 0:128]
    out_up = lambda: small_ref[0, :, 128:256]
    up_down = lambda: small_ref[0, :, 256:512]
    down_up = lambda: small_ref[0, :, 512:640]

    @pl.when(step == 0)
    def _():
        mask = mask_ref[...]
        z = z_ref[...]
        lat_out_ref[...] = (dot(z, out_down()) * mask).astype(BF)
        x2 = x_ref[...].astype(F32) + (dot(z, w_out_ref[0]) + dot(lat_out_ref[...], out_up(), NT))
        x2_ref[...] = x2
        normed, inv = norm_fwd(x2, gain_ref[...])
        inv_ref[...] = jnp.broadcast_to(inv, inv_ref.shape)
        h2_ref[...] = normed.astype(BF)
        latent = dot(h2_ref[...], up_down())
        lat_up_ref[:, :AR] = (latent[:, :AR] * mask).astype(BF)
        lat_up_ref[:, AR:] = (latent[:, AR:] * mask).astype(BF)
        dl_down_ref[...] = (dot(d_ref[...], down_up()) * mask).astype(BF)
        acc_ref[...] = jnp.zeros_like(acc_ref)
        lat_acc_ref[...] = jnp.zeros_like(lat_acc_ref)
        dh_ref[...] = jnp.zeros_like(dh_ref)
        dlat_ref[...] = jnp.zeros_like(dlat_ref)

    h2 = h2_ref[...]
    d = d_ref[...]
    w_gate, w_lift = w_up_ref[0, :, :FB], w_up_ref[0, :, FB:]
    lat0, lat1 = lat_up_ref[:, :AR], lat_up_ref[:, AR:]
    uu0, uu1 = wd1_ref[0, :, 256:384], wd1_ref[0, :, 384:512]
    dd = wd1_ref[0, :, 512:640]
    wda, wdb = wd0_ref[0], wd1_ref[0, :, :256]
    gate = dot(h2, w_gate) + dot(lat0, uu0, NT)
    lift = dot(h2, w_lift) + dot(lat1, uu1, NT)
    sig = jax.nn.sigmoid(gate)
    silu = gate * sig
    act = (silu * lift).astype(BF)
    acc_ref[:, :768] += dot(act, wda)
    acc_ref[:, 768:] += dot(act, wdb)
    lat_acc_ref[...] += dot(act, dd)
    d_act = dot(d[:, :768], wda, NT) + dot(d[:, 768:], wdb, NT) + dot(dl_down_ref[...], dd, NT)
    d_gate = (d_act * lift * (sig * (1.0 + gate * (1.0 - sig)))).astype(BF)
    d_lift = (d_act * silu).astype(BF)
    dh_ref[...] += dot(d_gate, w_gate, NT) + dot(d_lift, w_lift, NT)
    dlat_ref[:, :AR] += dot(d_gate, uu0)
    dlat_ref[:, AR:] += dot(d_lift, uu1)
    chips = FB // 48
    first = pl.multiple_of(step * chips, chips)
    for place, term in (
        (0, dot(d_gate, lat0, TN)),
        (1, dot(d_lift, lat1, TN)),
        (2, dot(act, dl_down_ref[...], TN)),
    ):
        shaped = term.reshape(chips, 3, 16, AR).astype(BF)
        for k in range(3):
            if place < 2:
                at = k * 256 + place * AR
                grads_ref[0, pl.ds(first, chips), :, at : at + AR] = shaped[:, k]
            else:
                grads_ref[1, pl.ds(first, chips), :, k * AR : (k + 1) * AR] = shaped[:, k]

    @pl.when(step == pl.num_programs(0) - 1)
    def _():
        mask = mask_ref[...]
        lat_down = (lat_acc_ref[...] * mask).astype(BF)
        out = (x2_ref[...] + acc_ref[...] + dot(lat_down, down_up(), NT)).astype(BF)
        for m in range(MB):
            s = slice(m * GROUP, (m + 1) * GROUP)
            back_ref[:, m * D : (m + 1) * D] = dot(place_ref[m], out[s], TN).astype(BF)
        d = d_ref[...]
        h2 = h2_ref[...]
        z = z_ref[...]

        def put(half, at, value):
            grads_ref[half, :, :, at : at + AR] = value.reshape(64, 16, AR).astype(BF)

        put(0, 768, dot(d, lat_down, TN))
        dlu0 = (dlat_ref[:, :AR] * mask).astype(BF)
        dlu1 = (dlat_ref[:, AR:] * mask).astype(BF)
        put(1, 640, dot(h2, dlu0, TN))
        put(1, 768, dot(h2, dlu1, TN))
        ud = up_down()
        dh = dh_ref[...] + (dot(dlu0, ud[:, :AR], NT) + dot(dlu1, ud[:, AR:], NT))
        dmid = d.astype(F32) + norm_bwd(dh, x2_ref[...], inv_ref[:, :1], gain_ref[...])
        dmid_ref[...] = dmid
        dmb = dmid.astype(BF)
        dlo = (dot(dmb, out_up()) * mask).astype(BF)
        put(1, 384, dot(z, dlo, TN))
        put(1, 512, dot(dmb, lat_out_ref[...], TN))
        dz_ref[...] = (dot(dmb, w_out_ref[0], NT) + dot(dlo, out_down(), NT)).astype(BF)


def ffn(x, d, z, gain, mask, place, a2, a3):
    whole = lambda *shape: pl.BlockSpec(shape, lambda j: (0,) * len(shape))
    return pl.pallas_call(
        ffn_kernel,
        grid=(FFP // FB,),
        out_shape=(
            jax.ShapeDtypeStruct((GROUP, MB * D), BF),
            jax.ShapeDtypeStruct((ROWS, D), BF),
            jax.ShapeDtypeStruct((ROWS, D), F32),
            jax.ShapeDtypeStruct((2, 64, 16, 896), BF),
        ),
        in_specs=[
            whole(ROWS, D),
            whole(ROWS, D),
            whole(ROWS, D),
            whole(1, D),
            whole(ROWS, AR),
            whole(MB, GROUP, GROUP),
            pl.BlockSpec((1, D, D), lambda j: (1, 0, 3)),
            pl.BlockSpec((1, D, D), lambda j: (0, 0, 3)),
            pl.BlockSpec((1, D, 2 * FB), lambda j: (j // 2, 0, j % 2)),
            pl.BlockSpec((1, FB, 768), lambda j: (0, j, 0)),
            pl.BlockSpec((1, FB, 768), lambda j: (1, j, 0)),
        ],
        out_specs=(
            whole(GROUP, MB * D),
            whole(ROWS, D),
            whole(ROWS, D),
            whole(2, 64, 16, 896),
        ),
        scratch_shapes=[
            pltpu.VMEM((ROWS, D), F32),
            pltpu.VMEM((ROWS, D), BF),
            pltpu.VMEM((ROWS, 128), F32),
            pltpu.VMEM((ROWS, AR), BF),
            pltpu.VMEM((ROWS, 2 * AR), BF),
            pltpu.VMEM((ROWS, AR), BF),
            pltpu.VMEM((ROWS, D), F32),
            pltpu.VMEM((ROWS, AR), F32),
            pltpu.VMEM((ROWS, D), F32),
            pltpu.VMEM((ROWS, 2 * AR), F32),
        ],
        compiler_params=pltpu.CompilerParams(vmem_limit_bytes=VMEM_LIMIT),
        name="ffn",
    )(x, d, z, gain, mask, place, a2, a2, a2, a3, a3)


def heads_bwd_kernel(
    split_ref, x_ref, gain_ref, mask_ref, place_ref, proj_ref, dz_ref, dmid_ref, h1_ref, lat_ref,
    w_ref, down_ref, up_ref, pers_ref, wf_ref, lw_ref,
    back_ref, grads_ref,
    dh_ref, dlat_ref,
):
    step = pl.program_id(0)

    @pl.when(step == 0)
    def _():
        dh_ref[...] = jnp.zeros_like(dh_ref)
        dlat_ref[...] = jnp.zeros_like(dlat_ref)

    pieces = [proj_ref[:, p * HEAD : (p + 1) * HEAD] for p in range(7)]
    q, k, v = (pieces[i].astype(BF) for i in range(3))
    pk, pv = pers_ref[0], pers_ref[1]
    near, far = attend(q, k, v, pk, pv, allowed_mask(split_ref))
    near_half = near.astype(BF)
    dz = dz_ref[...]
    d_near = by_group(lambda s, g: dot(dz[s], v[s], NT))
    d_far = dot(dz, pv, NT)
    d_v = by_group(lambda s, g: dot(near_half[s], dz[s], TN))
    total = jnp.sum(d_near * near, axis=-1, keepdims=True) + jnp.sum(
        d_far * far, axis=-1, keepdims=True
    )
    ds_near = (near * (d_near - total) * SCALE).astype(BF)
    ds_far = (far * (d_far - total) * SCALE).astype(BF)
    d_q = by_group(lambda s, g: dot(ds_near[s], k[s])) + dot(ds_far, pk)
    d_k = by_group(lambda s, g: dot(ds_near[s], q[s], TN))

    dzf = dz.astype(F32)
    opening = jax.nn.sigmoid(pieces[6])
    kn, k_inv = unit(pieces[3])
    qn, q_inv = unit(pieces[5])
    kept = memory_terms(kn, qn, pieces[4], wf_ref, lw_ref)
    mem = memory_out(kept)
    d_open = dzf * mem * (opening * (1.0 - opening))
    d_kn, d_qn, d_mv = memory_bwd(kept, dzf * opening)
    d_mk = unit_bwd(d_kn, pieces[3], k_inv)
    d_mq = unit_bwd(d_qn, pieces[5], q_inv)
    dy = [item.astype(BF) for item in (d_q, d_k, d_v, d_mk, d_mv, d_mq, d_open)]
    dh_ref[...] += dot(jnp.concatenate(dy, axis=1), w_ref[0], NT)
    first = pl.multiple_of(step * 8, 8)
    for part in range(7):
        s = slice(part * AR, (part + 1) * AR)
        dlat_ref[:, s] += dot(dy[part], up_ref[0, :, s])
        grads_ref[1, pl.ds(first, 8), :, s] = (
            dot(dy[part], lat_ref[:, s], TN).reshape(8, 16, AR).astype(BF)
        )

    @pl.when(step == pl.num_programs(0) - 1)
    def _():
        mask = mask_ref[...]
        dlat = jnp.concatenate(
            [(dlat_ref[:, p * AR : (p + 1) * AR] * mask).astype(BF) for p in range(7)], axis=1
        )
        grads_ref[0] = dot(h1_ref[...], dlat, TN).reshape(64, 16, 7 * AR).astype(BF)
        dh = dh_ref[...] + dot(dlat, down_ref[0], NT)
        x = x_ref[...].astype(F32)
        inv = lax.rsqrt(jnp.mean(x * x, axis=-1, keepdims=True) + EPS)
        dx = (dmid_ref[...] + norm_bwd(dh, x, inv, gain_ref[...])).astype(BF)
        for m in range(MB):
            s = slice(m * GROUP, (m + 1) * GROUP)
            back_ref[:, m * D : (m + 1) * D] = dot(place_ref[m], dx[s], TN).astype(BF)


def heads_bwd(split, x, gain, mask, place, proj, dz, dmid, h1, lat, a1, persistent, wf, lw):
    whole = lambda *shape: pl.BlockSpec(shape, lambda h: (0,) * len(shape))
    return pl.pallas_call(
        heads_bwd_kernel,
        grid=(H,),
        out_shape=(
            jax.ShapeDtypeStruct((GROUP, MB * D), BF),
            jax.ShapeDtypeStruct((2, 64, 16, 896), BF),
        ),
        in_specs=[
            pl.BlockSpec(memory_space=pltpu.SMEM),
            whole(ROWS, D),
            whole(1, D),
            whole(ROWS, AR),
            whole(MB, GROUP, GROUP),
            pl.BlockSpec((ROWS, HCOLS), lambda h: (0, h)),
            pl.BlockSpec((ROWS, HEAD), lambda h: (0, h)),
            whole(ROWS, D),
            whole(ROWS, D),
            whole(ROWS, 7 * AR),
            pl.BlockSpec((1, D, HCOLS), lambda h: (h // 4, 0, h % 4)),
            pl.BlockSpec((1, D, HCOLS), lambda h: (0, 0, 4)),
            pl.BlockSpec((1, HEAD, HCOLS), lambda h: (1, h, 4)),
            pl.BlockSpec((2, NP, HEAD), lambda h: (0, 0, h)),
            pl.BlockSpec((1, MB, GROUP, GROUP), lambda h: (h, 0, 0, 0)),
            pl.BlockSpec((1, MB, 8, GROUP), lambda h: (h, 0, 0, 0)),
        ],
        out_specs=(whole(GROUP, MB * D), whole(2, 64, 16, 896)),
        scratch_shapes=[pltpu.VMEM((ROWS, D), F32), pltpu.VMEM((ROWS, 7 * AR), F32)],
        compiler_params=pltpu.CompilerParams(vmem_limit_bytes=VMEM_LIMIT),
        name="heads_bwd",
    )(split, x, gain, mask, place, proj, dz, dmid, h1, lat, a1, a1, a1, persistent, wf, lw)


def by_rank(value, parts):
    rows = value.shape[1]
    return value.reshape(NAD, rows, parts, R).transpose(1, 2, 0, 3).reshape(rows, parts * AR)


def by_rank_t(value, parts):
    cols = value.shape[2]
    return value.reshape(NAD, parts, R, cols).transpose(3, 1, 0, 2).reshape(cols, parts * AR)


def pack_shards(w_in, w_out, w_up, w_down, in_down, in_up, out_down, out_up, up_down, up_up, down_down, down_up):
    rows = w_in.shape[0]
    heads = w_in.reshape(rows, 7, H, HEAD).transpose(0, 2, 1, 3).reshape(rows, 2, 4 * HCOLS)
    a1 = jnp.stack(
        [
            jnp.concatenate([heads[:, 0], by_rank(in_down, 7)], axis=1),
            jnp.concatenate([heads[:, 1], by_rank_t(in_up, 7)], axis=1),
        ]
    )
    up = w_up.reshape(rows, 2, N_DEV, FF_SHARD)
    up = jnp.pad(up, ((0, 0), (0, 0), (0, 0), (0, FF_PAD - FF_SHARD)))
    up = up.reshape(rows, 2, FFP // FB, FB).transpose(0, 2, 1, 3).reshape(rows, 2, 4 * FB)
    small = jnp.concatenate(
        [by_rank(out_down, 1), by_rank_t(out_up, 1), by_rank(up_down, 2), by_rank_t(down_up, 1)], axis=1
    )
    small = jnp.pad(small, ((0, 0), (0, D - small.shape[1])))
    a2 = jnp.stack(
        [jnp.concatenate([up[:, 0], small], axis=1), jnp.concatenate([up[:, 1], w_out], axis=1)]
    )
    rest = jnp.concatenate([w_down[:, 768:], by_rank_t(up_up, 2), by_rank(down_down, 1)], axis=1)
    rest = jnp.pad(rest, ((0, 0), (0, 128)))
    a3 = jnp.stack([w_down[:, :768], rest])
    a3 = jnp.pad(a3, ((0, 0), (0, FF_PAD - FF_SHARD), (0, 0)))
    return a1, a2, a3


def un_rank(value, parts):
    rows = value.shape[0]
    return value.reshape(rows, parts, NAD, R).transpose(2, 0, 1, 3).reshape(NAD, rows, parts * R)


def un_rank_t(value, parts):
    cols = value.shape[0]
    return value.reshape(cols, parts, NAD, R).transpose(2, 1, 3, 0).reshape(NAD, parts * R, cols)


def unpack_grads(ffn_chip, heads_chip, core):
    def rows8(value):
        return lax.dynamic_slice_in_dim(value, core * 8, 8, axis=0)

    grad_id = un_rank(rows8(heads_chip[0]), 7)
    grad_iu = un_rank_t(rows8(heads_chip[1]), 7)
    tall = lambda value, width: value.reshape(16, 3, width).transpose(1, 0, 2).reshape(48, width)

    def rows22(value):
        return lax.dynamic_slice_in_dim(value, core * FF_PAD, FF_PAD, axis=0)[:FF_SHARD]

    grad_uu = un_rank_t(rows22(tall(ffn_chip[0, :, :768], 256)), 2)
    grad_dd = un_rank(rows22(tall(ffn_chip[1, :, :384], AR)), 1)
    grad_du = un_rank_t(rows8(ffn_chip[0, :, 768:]), 1)
    grad_od = un_rank(rows8(ffn_chip[1, :, 384:512]), 1)
    grad_ou = un_rank_t(rows8(ffn_chip[1, :, 512:640]), 1)
    grad_ud = un_rank(rows8(ffn_chip[1, :, 640:896]), 2)
    return grad_id, grad_iu, grad_od, grad_ou, grad_ud, grad_uu, grad_dd, grad_du


def local_layer(x, d, dec, dec_t, lengths, ids, gain_mix, gain_ffn, persistent, place, a1, a2, a3):
    split = (lengths[:, 0] < GROUP).astype(F32)
    row_ids = jnp.where(
        (jnp.arange(GROUP)[None, :] >= lengths[:, :1]), ids[:, 1:], ids[:, :1]
    ).reshape(ROWS)
    mask = (row_ids[:, None] == (jnp.arange(AR) // R)[None, :]).astype(F32)
    gain_mix, gain_ffn = gain_mix[None, :], gain_ffn[None, :]
    wf, lw = decay_weights(1.0 - split, dec, dec_t)
    proj, z, h1, lat = heads_fwd(split, x, gain_mix, mask, a1, persistent, wf, lw)
    back, dz, dmid, grads_ffn = ffn(x, d, z, gain_ffn, mask, place, a2, a3)
    back_grad, grads_heads = heads_bwd(
        split, x, gain_mix, mask, place, proj, dz, dmid, h1, lat, a1, persistent, wf, lw
    )
    return back, back_grad, grads_ffn, grads_heads
MESH = pl.DeviceIdType.MESH


def position():
    me = lax.axis_index("fsdp")
    chip = me // 2
    return me % 2, (chip // 16, (chip // 4) % 4, chip % 4)


def device(core, spot):
    return (((spot[0] * 4 + spot[1]) * 4 + spot[2]) * 2 + core,)


def moved(spot, axis, by):
    return tuple((v + by + 4) % 4 if i == axis else v for i, v in enumerate(spot))


def cut(lanes, count):
    base, extra = divmod(lanes, count)
    runs, at = [], 0
    for i in range(count):
        size = base + (1 if i < extra else 0)
        runs.append((at * 128, size * 128))
        at += size
    return runs


class Sends:
    def __init__(self, send_sem, recv_sem):
        self.send_sem, self.recv_sem = send_sem, recv_sem
        self.slots, self.open = {}, []

    def copy(self, name, src, dst, target):
        slot = self.slots.setdefault(name, len(self.slots))
        return pltpu.make_async_remote_copy(
            src_ref=src, dst_ref=dst, send_sem=self.send_sem.at[slot], recv_sem=self.recv_sem.at[slot],
            device_id=target, device_id_type=MESH,
        )

    def start(self, name, src, dst, target):
        copy = self.copy(name, src, dst, target)
        copy.start()
        self.open.append(copy)

    def arrived(self, name, ref, target):
        self.copy(name, ref, ref, target).wait_recv()

    def drain(self):
        for copy in self.open:
            copy.wait_send()
        self.open = []


def greet(targets):
    barrier = pltpu.get_barrier_semaphore()
    for target in targets:
        pl.semaphore_signal(barrier, inc=1, device_id=target, device_id_type=MESH)
    pl.semaphore_wait(barrier, len(targets))


def gather_kernel(shapes, *refs):
    n = len(shapes)
    mine, outs = refs[:n], refs[n : 2 * n]
    inc, stage = refs[2 * n : 3 * n], refs[3 * n : 4 * n]
    send_sem, recv_sem, local_sem = refs[4 * n :]
    core, spot = position()
    sibling = device(1 - core, spot)
    sends = Sends(send_sem, recv_sem)
    greet([sibling] + [device(core, moved(spot, a, by)) for a in range(3) for by in (1, -1)])

    for i in range(n):
        sends.start(("pair", i), mine[i].at[1 - core], inc[i], sibling)
    for i in range(n):
        sends.arrived(("pair", i), inc[i], sibling)
        own, other = mine[i][core], inc[i][...]
        first = jnp.where(core == 0, own, other)
        last = jnp.where(core == 0, other, own)
        stage[i][...] = jnp.concatenate([first, last], axis=0).astype(BF)
        pltpu.make_async_copy(
            stage[i], outs[i].at[core, spot[0], spot[1], spot[2]], local_sem.at[i]
        ).start()
    for i in range(n):
        pltpu.make_async_copy(
            stage[i], outs[i].at[core, spot[0], spot[1], spot[2]], local_sem.at[i]
        ).wait()

    def block(i, whole_axes, spot_at, cols, half=None):
        index = [
            pl.ds(0, 4) if a in whole_axes else pl.ds(spot_at[a], 1) for a in range(3)
        ]
        half = core if half is None else half
        return outs[i].at[half, index[0], index[1], index[2], :, pl.ds(cols[0], cols[1])]

    jobs = [
        (i, part, cols)
        for i in range(n)
        for part, cols in enumerate(cut(shapes[i][1] // 128, 3))
    ]

    def two(cols):
        runs = cut(cols[1] // 128, 2)
        return [(cols[0] + at, size) for at, size in runs]

    forwards = []

    def forward(name, i, whole_axes, spot_at, cols):
        ref = block(i, whole_axes, spot_at, cols)
        sends.start(name, ref, ref, sibling)
        forwards.append((name, i, whole_axes, spot_at, cols))

    for phase in range(3):
        for i, part, cols in jobs:
            axis = (part + phase) % 3
            done = [(part + p) % 3 for p in range(phase)]
            right, left = device(core, moved(spot, axis, 1)), device(core, moved(spot, axis, -1))
            parts = two(cols)
            for step, (to_right, to_left) in enumerate(((0, 1), (1, 0))):
                ref = block(i, done, spot, parts[to_right])
                sends.start((i, part, phase, "r", step), ref, ref, right)
                ref = block(i, done, spot, parts[to_left])
                sends.start((i, part, phase, "l", step), ref, ref, left)
            if phase == 2:
                forward((i, part, "f"), i, done, spot, cols)
        for i, part, cols in jobs:
            axis = (part + phase) % 3
            done = [(part + p) % 3 for p in range(phase)]
            right, left = device(core, moved(spot, axis, 1)), device(core, moved(spot, axis, -1))
            at_left, at_right = moved(spot, axis, -1), moved(spot, axis, 1)
            parts = two(cols)
            ref = block(i, done, at_left, parts[0])
            sends.arrived((i, part, phase, "r", 0), ref, left)
            sends.start((i, part, phase, "r", 2), ref, ref, right)
            if phase == 2:
                forward((i, part, "f", 0), i, done, at_left, parts[0])
            ref = block(i, done, at_right, parts[1])
            sends.arrived((i, part, phase, "l", 0), ref, right)
            sends.start((i, part, phase, "l", 2), ref, ref, left)
            if phase == 2:
                forward((i, part, "f", 1), i, done, at_right, parts[1])
        for i, part, cols in jobs:
            axis = (part + phase) % 3
            done = [(part + p) % 3 for p in range(phase)]
            right, left = device(core, moved(spot, axis, 1)), device(core, moved(spot, axis, -1))
            at_left, at_right = moved(spot, axis, -1), moved(spot, axis, 1)
            far = moved(spot, axis, 2)
            parts = two(cols)
            for k, (name, at, cc, source) in enumerate(
                (
                    (("r", 1), at_left, parts[1], left),
                    (("l", 1), at_right, parts[0], right),
                    (("r", 2), far, parts[0], left),
                    (("l", 2), far, parts[1], right),
                )
            ):
                sends.arrived((i, part, phase) + name, block(i, done, at, cc), source)
                if phase == 2:
                    forward((i, part, "f", 2 + k), i, done, at, cc)
    for name, i, whole_axes, spot_at, cols in forwards:
        sends.arrived(name, block(i, whole_axes, spot_at, cols, 1 - core), sibling)
    sends.drain()


def gather(mine, collective_id):
    shapes = [(m.shape[1], m.shape[2]) for m in mine]
    n = len(shapes)
    slots = n * (1 + 3 * (3 * 6 + 7))
    return pl.pallas_call(
        functools.partial(gather_kernel, shapes),
        out_shape=tuple(
            jax.ShapeDtypeStruct((2, 4, 4, 4, 2 * r, c), BF) for r, c in shapes
        ),
        in_specs=[pl.BlockSpec(memory_space=pltpu.VMEM)] * n,
        out_specs=tuple(pl.BlockSpec(memory_space=pl.ANY) for _ in shapes),
        scratch_shapes=[pltpu.VMEM((r, c), F32) for r, c in shapes]
        + [pltpu.VMEM((2 * r, c), BF) for r, c in shapes]
        + [
            pltpu.SemaphoreType.DMA((slots,)),
            pltpu.SemaphoreType.DMA((slots,)),
            pltpu.SemaphoreType.DMA((n,)),
        ],
        compiler_params=pltpu.CompilerParams(
            collective_id=collective_id, has_side_effects=True, vmem_limit_bytes=VMEM_LIMIT
        ),
        name="gather",
    )(*mine)


def scatter_kernel(count, *refs):
    g_refs, out_refs = refs[:count], refs[count : 2 * count]
    inc0, total, inc1, inc2, inc3, t1, t2 = refs[2 * count : 2 * count + 7]
    send_sem, recv_sem = refs[2 * count + 7 :]
    core, spot = position()
    sibling = device(1 - core, spot)
    sends = Sends(send_sem, recv_sem)
    peers = [(a, by) for a in range(3) for by in (1, 3, 2)]
    greet([sibling] + [device(core, moved(spot, a, by)) for a, by in peers])
    parts = cut(7, 3)
    for i in range(count):
        for x in range(4):
            sends.start((i, "pair", x), g_refs[i].at[1 - core, pl.ds(16 * x, 16)], inc0.at[i, x], sibling)
    for i in range(count):
        for x in range(4):
            sends.arrived((i, "pair", x), inc0.at[i, x], sibling)
            both = g_refs[i][core, pl.ds(16 * x, 16)].astype(F32) + inc0[i, x].astype(F32)
            total[i, x] = both.reshape(4, 4, 16, 896).astype(BF)

    def index(done, axis, at):
        return tuple(
            spot[a] if a in done else (at if a == axis else slice(None)) for a in range(3)
        )

    def squeeze(done, axis, a_order):
        return [a for a in range(3) if a not in done and a != axis]

    jobs = [(i, part, cols) for i in range(count) for part, cols in enumerate(parts)]
    for i, part, cols in jobs:
        axis = part
        cs = pl.ds(cols[0], cols[1])
        for k, by in enumerate((2, 1, 3)):
            to = moved(spot, axis, by)
            idx = index((), axis, to[axis])
            sends.start((i, part, 1, by), total.at[(i,) + idx + (slice(None), cs)], inc1.at[i, k, :, :, :, cs], device(core, to))
    for i, part, cols in jobs:
        axis = part
        cs = pl.ds(cols[0], cols[1])
        idx = index((), axis, spot[axis])
        acc = total[(i,) + idx + (slice(None), cs)].astype(F32)
        for k, by in enumerate((2, 1, 3)):
            frm = moved(spot, axis, -by)
            sends.arrived((i, part, 1, by), inc1.at[i, k, :, :, :, cs], device(core, frm))
            acc = acc + inc1[i, k, :, :, :, cs].astype(F32)
        t1[i, :, :, :, cs] = acc.astype(BF)
        axis2 = (part + 1) % 3
        rest = [a for a in range(3) if a != axis]
        for k, by in enumerate((2, 1, 3)):
            to = moved(spot, axis2, by)
            src = t1.at[i, to[axis2], :, :, cs] if rest[0] == axis2 else t1.at[i, :, to[axis2], :, cs]
            sends.start((i, part, 2, by), src, inc2.at[i, k, :, :, cs], device(core, to))
    for i, part, cols in jobs:
        axis2, axis3 = (part + 1) % 3, (part + 2) % 3
        rest = [a for a in range(3) if a != part]
        cs = pl.ds(cols[0], cols[1])
        own = spot[axis2]
        acc = (t1[i, own, :, :, cs] if rest[0] == axis2 else t1[i, :, own, :, cs]).astype(F32)
        for k, by in enumerate((2, 1, 3)):
            frm = moved(spot, axis2, -by)
            sends.arrived((i, part, 2, by), inc2.at[i, k, :, :, cs], device(core, frm))
            acc = acc + inc2[i, k, :, :, cs].astype(F32)
        t2[i, :, :, cs] = acc.astype(BF)
        for k, by in enumerate((2, 1, 3)):
            to = moved(spot, axis3, by)
            sends.start((i, part, 3, by), t2.at[i, to[axis3], :, cs], inc3.at[i, k, :, cs], device(core, to))
    for i, part, cols in jobs:
        axis3 = (part + 2) % 3
        cs = pl.ds(cols[0], cols[1])
        acc = t2[i, spot[axis3], :, cs].astype(F32)
        for k, by in enumerate((2, 1, 3)):
            frm = moved(spot, axis3, -by)
            sends.arrived((i, part, 3, by), inc3.at[i, k, :, cs], device(core, frm))
            acc = acc + inc3[i, k, :, cs].astype(F32)
        out_refs[i][core, :, cs] = acc
    for i in range(count):
        sends.start((i, "last"), out_refs[i].at[core], out_refs[i].at[core], sibling)
    for i in range(count):
        sends.arrived((i, "last"), out_refs[i].at[1 - core], sibling)
    sends.drain()


def scatter(grads, collective_id):
    n = len(grads)
    slots = n * (4 + 3 * 9 + 1)
    return pl.pallas_call(
        functools.partial(scatter_kernel, n),
        out_shape=tuple(jax.ShapeDtypeStruct((2, 16, 896), F32) for _ in grads),
        in_specs=[pl.BlockSpec(memory_space=pltpu.VMEM)] * n,
        out_specs=tuple(pl.BlockSpec(memory_space=pltpu.VMEM) for _ in grads),
        scratch_shapes=[
            pltpu.VMEM((n, 4, 16, 16, 896), BF),
            pltpu.VMEM((n, 4, 4, 4, 16, 896), BF),
            pltpu.VMEM((n, 3, 4, 4, 16, 896), BF),
            pltpu.VMEM((n, 3, 4, 16, 896), BF),
            pltpu.VMEM((n, 3, 16, 896), BF),
            pltpu.VMEM((n, 4, 4, 16, 896), BF),
            pltpu.VMEM((n, 4, 16, 896), BF),
            pltpu.SemaphoreType.DMA((slots,)),
            pltpu.SemaphoreType.DMA((slots,)),
        ],
        compiler_params=pltpu.CompilerParams(
            collective_id=collective_id, has_side_effects=True, vmem_limit_bytes=VMEM_LIMIT
        ),
        name="scatter",
    )(*grads)


def body(
    tokens, cotangent, decays, route, lengths, adapter_ids, gain_mix, gain_ffn, persistent,
    w_in, w_out, w_up, w_down, in_down, in_up, out_down, out_up, up_down, up_up, down_down, down_up,
):
    me = lax.axis_index("fsdp")
    packed = pack_shards(
        w_in, w_out, w_up, w_down, in_down, in_up, out_down, out_up, up_down, up_up, down_down, down_up
    )
    a1, a2, a3 = gather([item.astype(F32) for item in packed], 0)
    a1 = a1.reshape(2, D, a1.shape[-1])
    a2 = a2.reshape(2, D, a2.shape[-1])
    a3 = a3.reshape(2, FFP, a3.shape[-1])

    spots = jnp.arange(GROUP, dtype=jnp.int32)
    own = lax.dynamic_slice_in_dim(route, me * GROUP, GROUP, axis=1)
    send = (own[:, None, :] // GROUP == spots[None, :, None]).astype(BF)
    blocks = route.reshape(MB, N_DEV, GROUP)
    landing = jnp.sum(jnp.where(blocks // GROUP == me, blocks % GROUP, 0), axis=2)
    place = (landing[:, None, :] == spots[None, :, None]).astype(BF)

    def permute(onehot, values):
        return jnp.einsum("mij,mjd->mid", onehot, values, preferred_element_type=F32).astype(BF)

    def exchange(values):
        return lax.all_to_all(values, "fsdp", split_axis=0, concat_axis=0, tiled=True)

    out_x = permute(send, tokens)
    out_d = permute(send, cotangent)
    out_r = permute(send, decays)
    sent = jnp.concatenate(
        [out_x[0], out_x[1], out_d[0], out_d[1], out_r[0], out_r[1], jnp.zeros((GROUP, 80), BF)], axis=1
    )
    got = exchange(sent)
    at = lambda lo, width: jnp.stack([got[:, lo : lo + width], got[:, lo + width : lo + 2 * width]])
    x = permute(place, at(0, D)).reshape(ROWS, D)
    d = permute(place, at(2 * D, D)).reshape(ROWS, D)
    dec = permute(place, at(4 * D, 3 * H)).astype(F32).reshape(ROWS, 3 * H)
    back, back_grad, grads_ffn, grads_heads = local_layer(
        x, d, dec, dec.T, lengths[:, 0], adapter_ids[:, 0], gain_mix, gain_ffn, persistent, place, a1, a2, a3
    )

    def home(values):
        values = exchange(values)
        return jnp.einsum(
            "mij,mid->mjd", send, values.reshape(GROUP, MB, D).transpose(1, 0, 2), preferred_element_type=F32
        ).astype(BF)

    ffn_chip, heads_chip = scatter([grads_ffn, grads_heads], 1)
    return (home(back), home(back_grad)) + unpack_grads(ffn_chip, heads_chip, me % 2)


def solution(mesh):
    rows, cols = P(None, "fsdp", None), P(None, None, "fsdp")
    weight = P("fsdp", None)
    return jax.shard_map(
        body,
        mesh=mesh,
        in_specs=(rows, rows, rows, P(), rows, rows, P(), P(), P())
        + (weight,) * 4
        + (rows, cols) * 4,
        out_specs=(rows, rows) + (rows, cols) * 4,
        check_vma=False,
    )
```

time: 5370 us -> 320 us (0.06)
  waiting for transfers between devices: 4490 us -> 14.7 us
  matrix products: 251 us -> 7.47 us
  Pallas kernels: 0 us -> 239 us
  blocking collectives: 201 us -> 0 us
  local copies, waits for them, and re-layouts: 211 us -> 26.7 us
  other arithmetic: 103 us -> 9.02 us
    reduce_scatter x7 -> x0, waiting for transfers between devices: 4430 us -> none  [the longest x1 654 us: body(): lax.psum_scatter(totals[5], 'fsdp', scatter_dimension=2, tiled=True)]
    dot_general x188 -> x8, matrix products: 248 us -> 7.47 us  [the longest x6 5.19 us: permute(): jnp.einsum('mij,mjd->mid', onehot, values, preferred_element_type=F32)]
    pallas_call x0 -> x6, Pallas kernels: none -> 239 us  [the longest x1 111 us: gather(): pl.pallas_call(functools.partial(gather_kernel, shapes), out_shape=tuple(...]
    all_gather x5 -> x0, blocking collectives: 201 us -> none  [the longest x1 43.4 us: body(): lax.all_gather(out_down, 'fsdp', axis=1, tiled=True)]
    unnamed x738 -> x53, local copies, waits for them, and re-layouts: 82.3 us -> 10.1 us
  transfers between devices with their start and end apart: 25 -> 3, of which waited for: 13 -> 2; matrix products, arithmetic and copies ran while one was open for 7% -> 7% of each run, Pallas kernels for 0% -> 35%
where the time goes in v1:
time: 320 us; the launch traced here: 319 us
  Pallas kernels  239 us (75%)
  local copies, waits for them, and re-layouts  26.7 us (8%)
  starting transfers between devices  21.2 us (7%)
  waiting for transfers between devices  14.7 us (5%)
  other arithmetic  9.02 us (3%)
  matrix products  7.47 us (2%)
    pallas_call x1, Pallas kernels, gather(): pl.pallas_call(functools.partial(gather_kernel, shapes), out_shape=tuple(...  111 us
    pallas_call x1, Pallas kernels, scatter(): pl.pallas_call(functools.partial(scatter_kernel, n), out_shape=tuple((jax...  41.6 us
    pallas_call x1, Pallas kernels, heads_bwd(): pl.pallas_call(heads_bwd_kernel, grid=(H,), out_shape=(jax.ShapeDtypeStru...  33.9 us
    pallas_call x1, Pallas kernels, ffn(): pl.pallas_call(ffn_kernel, grid=(FFP // FB,), out_shape=(jax.ShapeDtypeSt...  28.2 us
    all_to_all x3, starting transfers between devices, exchange(): lax.all_to_all(values, 'fsdp', split_axis=0, concat_axis=0, tiled=True)  21.2 us
    pallas_call x1, Pallas kernels, heads_fwd(): pl.pallas_call(heads_fwd_kernel, grid=(H,), out_shape=(jax.ShapeDtypeStru...  19.8 us
    all_to_all x3, waiting for transfers between devices, exchange(): lax.all_to_all(values, 'fsdp', split_axis=0, concat_axis=0, tiled=True)  14.7 us
    unnamed x53, local copies, waits for them, and re-layouts  10.1 us
  transfers between devices with their start and end apart: 3, of which 2 were waited for; matrix products, arithmetic and copies ran while one was open for 7% of the time, Pallas kernels for 35%

profile of v1, /device:TPU:1, one launch (start us, length us, event | category | flops | bytes accessed | tf_op | source)
XLA Modules:
  0.0 319.3 jit_solution(13337990895324005849)
XLA Ops:
  2.1 1.5 convolution_convert_fusion.5
  4.7 1.1 concatenate.21
  6.3 1.4 reduce.6
  7.7 1.6 reshape.304
  9.3 11.5 %all-to-all-start = ((bf16[128,2,2112]{2,1,0:T(2,128)(2,1)}), bf16[128,2,2112]{2,1,0:T(2,128)(2,1)S(1)}, u32[]{:S(2)}, u32[]{:S(2)}) async-start(bf16[128,2,2112]{2,1,0:T(2,128)(2,1)} %reshape.304), calls=%async_computation | async-start | bytes 2228224 | tf_op jit(solution)/shard_map/all_to_all | solution.py:912
  21.6 1.3 reshape.256
  28.6 111.1 %gather.1 = (bf16[2,4,4,4,16,4480]{5,4,3,2,1,0:T(8,128)(2,1)}, bf16[2,4,4,4,16,4096]{5,4,3,2,1,0:T(8,128)(2,1)}, bf16[2,4,4,4,48,768]{5,4,3,2,1,0:T(8,128)(2,1)}) custom-call(f32[2,8,4480]{2,1,0:T(8,128)} %maximum_convert_fusion.refs_0_, f32[2,8,4096]{2,1,0:T(8,128)} %maximum_convert_fusion.1.refs_1_, f32[2,24,768]{2,1,0:T(8,128)} %fusion.21.refs_2_), custom_call_target="tpu_custom_call" | custom-call | tf_op jit(solution)/shard_map/gather/pallas_call | solution.py:760
  141.9 1.2 reshape.305
  144.5 1.1 convolution_convert_fusion.3
  145.6 1.1 convolution_convert_fusion.2
  146.7 4.0 %decays.1 = (f32[8,2,128,128]{3,2,1,0:T(8,128)}, f32[8,2,8,128]{3,2,1,0:T(8,128)}) custom-call(f32[2]{0:T(128)} %broadcast_subtract_fusion.keep_ref, f32[256,24]{1,0:T(8,128)} %copy.177.dec_ref, f32[24,256]{1,0:T(8,128)} %bitcast.210), custom_call_target="tpu_custom_call" | custom-call | tf_op jit(solution)/shard_map/decays/pallas_call | solution.py:100
  150.8 19.8 %heads_fwd.1 = (f32[256,7168]{1,0:T(8,128)}, bf16[256,1024]{1,0:T(8,128)(2,1)}, bf16[256,1024]{1,0:T(8,128)(2,1)}, bf16[256,896]{1,0:T(8,128)(2,1)}) custom-call(f32[2]{0:T(128)} %compare_convert_fusion.1.split_ref, bf16[256,1024]{1,0:T(8,128)(2,1)} %bitcast.186, f32[1,1024]{1,0:T(1,128)} %bitcast.221, f32[256,128]{1,0:T(8,128)} %compare_convert_fusion.mask_ref, ...), custom_call_target="tpu_custom_call" | custom-call | tf_op jit(solution)/shard_map/heads_fwd/pallas_call | solution.py:238
  170.6 28.2 %ffn.1 = (bf16[128,2048]{1,0:T(8,128)(2,1)}, bf16[256,1024]{1,0:T(8,128)(2,1)}, f32[256,1024]{1,0:T(8,128)}, bf16[2,64,16,896]{3,2,1,0:T(8,128)(2,1)}) custom-call(bf16[256,1024]{1,0:T(8,128)(2,1)} %bitcast.187, bf16[256,1024]{1,0:T(8,128)(2,1)} %bitcast.192, bf16[256,1024]{1,0:T(8,128)(2,1)} %get-tuple-element.30.z_ref, f32[1,1024]{1,0:T(1,128)} %bitcast.227, ...), custom_call_target="tpu_custom_call" | custom-call | tf_op jit(solution)/shard_map/ffn/pallas_call | solution.py:369
  198.8 33.9 %heads_bwd.1 = (bf16[128,2048]{1,0:T(8,128)(2,1)}, bf16[2,64,16,896]{3,2,1,0:T(8,128)(2,1)}) custom-call(f32[2]{0:T(128)} %compare_convert_fusion.1.split_ref, bf16[256,1024]{1,0:T(8,128)(2,1)} %bitcast.188, f32[1,1024]{1,0:T(1,128)} %bitcast.222, f32[256,128]{1,0:T(8,128)} %compare_convert_fusion.mask_ref, bf16[2,128,128]{2,1,0:T(8,128)(2,1)} %fusion.16.place_ref, ...), custom_call_target="tpu_custom_call" | custom-call | tf_op jit(solution)/shard_map/heads_bwd/pallas_call | solution.py:482
  232.8 41.6 %scatter.1 = (f32[2,16,896]{2,1,0:T(8,128)}, f32[2,16,896]{2,1,0:T(8,128)}) custom-call(bf16[2,64,16,896]{3,2,1,0:T(8,128)(2,1)} %get-tuple-element.40.refs_0_, bf16[2,64,16,896]{3,2,1,0:T(8,128)(2,1)} %get-tuple-element.41.refs_1_), custom_call_target="tpu_custom_call" | custom-call | tf_op jit(solution)/shard_map/scatter/pallas_call | solution.py:865
  277.7 1.0 reduce.8
  278.7 1.2 reshape.308
  279.8 5.0 %all-to-all-start.2 = ((bf16[128,2,1024]{2,1,0:T(2,128)(2,1)}), bf16[128,2,1024]{2,1,0:T(2,128)(2,1)S(1)}, u32[]{:S(2)}, u32[]{:S(2)}) async-start(bf16[128,2,1024]{2,1,0:T(2,128)(2,1)} %reshape.308), calls=%async_computation.2 | async-start | bytes 1048576 | tf_op jit(solution)/shard_map/all_to_all | solution.py:912
  285.8 1.2 reshape.306
  287.8 10.6 %all-to-all-done.2 = bf16[128,2,1024]{2,1,0:T(2,128)(2,1)S(1)} async-done(((bf16[128,2,1024]{2,1,0:T(2,128)(2,1)}), bf16[128,2,1024]{2,1,0:T(2,128)(2,1)S(1)}, u32[]{:S(2)}, u32[]{:S(2)}) %all-to-all-start.2) | async-done | bytes 524320 | tf_op jit(solution)/shard_map/all_to_all | solution.py:912
  298.3 4.8 %all-to-all-start.1 = ((bf16[128,2,1024]{2,1,0:T(2,128)(2,1)}), bf16[128,2,1024]{2,1,0:T(2,128)(2,1)S(1)}, u32[]{:S(2)}, u32[]{:S(2)}) async-start(bf16[128,2,1024]{2,1,0:T(2,128)(2,1)} %reshape.306), calls=%async_computation.1 | async-start | bytes 1048576 | tf_op jit(solution)/shard_map/all_to_all | solution.py:912
  311.4 1.1 convolution_convert_fusion
  312.5 4.1 %all-to-all-done.1 = bf16[128,2,1024]{2,1,0:T(2,128)(2,1)S(1)} async-done(((bf16[128,2,1024]{2,1,0:T(2,128)(2,1)}), bf16[128,2,1024]{2,1,0:T(2,128)(2,1)S(1)}, u32[]{:S(2)}, u32[]{:S(2)}) %all-to-all-start.1) | async-done | bytes 524320 | tf_op jit(solution)/shard_map/all_to_all | solution.py:912
  318.2 1.1 convolution_convert_fusion.1
  (148 shorter events, 27.5 us)
Async XLA Ops:
  0.6 1.1 copy-start
  7.7 13.2 %copy-start.18 = (s32[2,1,2]{2,1,0:T(1,128)S(1)}, s32[2,1,2]{2,1,0:T(1,128)}, u32[]{:S(2)}) copy-start(s32[2,1,2]{2,1,0:T(1,128)} %param.26) | copy-start | bytes 52
  7.7 13.2 %copy-start.19 = (s32[2,1,2]{2,1,0:T(1,128)S(1)}, s32[2,1,2]{2,1,0:T(1,128)}, u32[]{:S(2)}) copy-start(s32[2,1,2]{2,1,0:T(1,128)} %param.25) | copy-start | bytes 52
  7.7 13.9 %copy-start.7 = (bf16[8,5632]{1,0:T(8,128)(2,1)S(1)}, bf16[8,5632]{1,0:T(8,128)(2,1)}, u32[]{:S(2)}) copy-start(bf16[8,5632]{1,0:T(8,128)(2,1)} %param.32) | copy-start | bytes 270340
  9.3 14.7 %copy-start.11 = (bf16[8,8,32]{2,1,0:T(8,128)(2,1)S(1)}, bf16[8,8,32]{2,1,0:T(8,128)(2,1)}, u32[]{:S(2)}) copy-start(bf16[8,8,32]{2,1,0:T(8,128)(2,1)} %param.38) | copy-start | bytes 12292
  9.3 132.6 %all-to-all-start = ((bf16[128,2,2112]{2,1,0:T(2,128)(2,1)}), bf16[128,2,2112]{2,1,0:T(2,128)(2,1)S(1)}, u32[]{:S(2)}, u32[]{:S(2)}) async-start(bf16[128,2,2112]{2,1,0:T(2,128)(2,1)} %reshape.304), calls=%async_computation | async-start | bytes 2228224 | tf_op jit(solution)/shard_map/all_to_all | solution.py:912
  20.8 3.4 %copy-start.14 = (bf16[8,8,16]{2,1,0:T(8,128)(2,1)S(1)}, bf16[8,8,16]{2,1,0:T(8,128)(2,1)}, u32[]{:S(2)}) copy-start(bf16[8,8,16]{2,1,0:T(8,128)(2,1)} %param.36) | copy-start | bytes 6148
  20.8 3.5 %copy-start.15 = (bf16[8,16,8]{1,2,0:T(8,128)(2,1)S(1)}, bf16[8,16,8]{1,2,0:T(8,128)(2,1)}, u32[]{:S(2)}) copy-start(bf16[8,16,8]{1,2,0:T(8,128)(2,1)} %param.37) | copy-start | bytes 6148
  20.8 3.6 %copy-start.16 = (bf16[8,16,8]{1,2,0:T(8,128)(2,1)S(1)}, bf16[8,16,8]{1,2,0:T(8,128)(2,1)}, u32[]{:S(2)}) copy-start(bf16[8,16,8]{1,2,0:T(8,128)(2,1)} %param.41) | copy-start | bytes 6148
  20.9 3.7 %copy-start.6 = (bf16[8,7168]{1,0:T(8,128)(2,1)S(1)}, bf16[8,7168]{1,0:T(8,128)(2,1)}, u32[]{:S(2)}) copy-start(bf16[8,7168]{1,0:T(8,128)(2,1)} %param.30) | copy-start | bytes 344068
  21.6 3.3 %copy-start.12 = (bf16[8,8,112]{2,1,0:T(8,128)(2,1)S(1)}, bf16[8,8,112]{2,1,0:T(8,128)(2,1)}, u32[]{:S(2)}) copy-start(bf16[8,8,112]{2,1,0:T(8,128)(2,1)} %param.34) | copy-start | bytes 43012
  22.9 2.4 copy-start.13
  22.9 2.8 copy-start.9
  23.0 3.1 copy-start.10
  23.0 3.3 %copy-start.17 = (bf16[8,1024]{1,0:T(8,128)(2,1)S(1)}, bf16[8,1024]{1,0:T(8,128)(2,1)}, u32[]{:S(2)}) copy-start(bf16[8,1024]{1,0:T(8,128)(2,1)} %param.31) | copy-start | bytes 49156
  24.6 3.2 %copy-start.8 = (bf16[22,1024]{1,0:T(8,128)(2,1)S(1)}, bf16[22,1024]{1,0:T(8,128)(2,1)}, u32[]{:S(2)}) copy-start(bf16[22,1024]{1,0:T(8,128)(2,1)} %param.33) | copy-start | bytes 135172
  24.7 3.2 %slice-start = ((bf16[22,1024]{1,0:T(8,128)(2,1)}), bf16[22,256]{1,0:T(8,128)(2,1)S(1)}, s32[]{:S(2)}) async-start(bf16[22,1024]{1,0:T(8,128)(2,1)} %param.33), calls=%async_computation.3 | async-start | bytes 24576 | tf_op jit(solution)/shard_map/slice | solution.py:543
  25.1 114.5 %copy-start.5 = (s32[2,16384]{1,0:T(2,128)S(1)}, s32[2,16384]{1,0:T(2,128)}, u32[]{:S(2)}) copy-start(s32[2,16384]{1,0:T(2,128)} %param.24) | copy-start | bytes 393220
  143.7 3.0 copy-start.4
  232.8 44.9 %copy-start.3 = (bf16[128,2048]{1,0:T(8,128)(2,1)S(1)}, bf16[128,2048]{1,0:T(8,128)(2,1)}, u32[]{:S(2)}) copy-start(bf16[128,2048]{1,0:T(8,128)(2,1)} %get-tuple-element.39) | copy-start | bytes 1572868
  274.4 10.5 %copy-start.2 = (bf16[128,2048]{1,0:T(8,128)(2,1)S(1)}, bf16[128,2048]{1,0:T(8,128)(2,1)}, u32[]{:S(2)}) copy-start(bf16[128,2048]{1,0:T(8,128)(2,1)} %get-tuple-element.33) | copy-start | bytes 1572868
  279.8 18.5 %all-to-all-start.2 = ((bf16[128,2,1024]{2,1,0:T(2,128)(2,1)}), bf16[128,2,1024]{2,1,0:T(2,128)(2,1)S(1)}, u32[]{:S(2)}, u32[]{:S(2)}) async-start(bf16[128,2,1024]{2,1,0:T(2,128)(2,1)} %reshape.308), calls=%async_computation.2 | async-start | bytes 1048576 | tf_op jit(solution)/shard_map/all_to_all | solution.py:912
  298.3 18.3 %all-to-all-start.1 = ((bf16[128,2,1024]{2,1,0:T(2,128)(2,1)}), bf16[128,2,1024]{2,1,0:T(2,128)(2,1)S(1)}, u32[]{:S(2)}, u32[]{:S(2)}) async-start(bf16[128,2,1024]{2,1,0:T(2,128)(2,1)} %reshape.306), calls=%async_computation.1 | async-start | bytes 1048576 | tf_op jit(solution)/shard_map/all_to_all | solution.py:912
  316.6 2.7 copy-start.1

commit v2 on v1

v2 whole, which is shorter than its diff:
```python
import functools
import math

import jax
import jax.numpy as jnp
from jax import lax
from jax.experimental import pallas as pl
from jax.experimental.pallas import tpu as pltpu
from jax.sharding import PartitionSpec as P

D = 1024
H = 8
HEAD = 128
FF = 2816
R = 16
NAD = 8
NP = 16
SPAN = 64
GROUP = 128
MB = 2
ROWS = MB * GROUP
N_DEV = 128
AR = NAD * R
HCOLS = 7 * HEAD
FF_SHARD = FF // N_DEV
FF_PAD = 24
FFP = FF_PAD * N_DEV
FB = 768
EPS = 1e-05
SCALE = 1.0 / math.sqrt(HEAD)
VMEM_LIMIT = 60 * 1024 * 1024
BF = jnp.bfloat16
F32 = jnp.float32

NN = (((1,), (0,)), ((), ()))
NT = (((1,), (1,)), ((), ()))
TN = (((0,), (0,)), ((), ()))


def dot(left, right, dims=NN):
    return lax.dot_general(left, right, dims, preferred_element_type=F32)


def exact(left, right, dims=NN):
    return lax.dot_general(
        left, right, dims, precision=lax.Precision.HIGHEST, preferred_element_type=F32
    )


def halves(value):
    high = value.astype(BF)
    return high, (value - high.astype(F32)).astype(BF)


def dot3(left, right, dims=NN):
    lh, ll = left
    rh, rl = right
    return dot(lh, rh, dims) + (dot(lh, rl, dims) + dot(ll, rh, dims))


def norm_fwd(values, gain):
    inv = lax.rsqrt(jnp.mean(values * values, axis=-1, keepdims=True) + EPS)
    return values * inv * gain, inv


def norm_bwd(grad, values, inv, gain):
    scaled = grad * gain
    return inv * (scaled - values * (inv * inv * jnp.mean(values * scaled, axis=-1, keepdims=True)))


def decay_kernel(split_ref, dec_ref, dect_ref, wf_ref, lw_ref):
    rows = lax.broadcasted_iota(jnp.int32, (GROUP, GROUP), 0)
    cols = lax.broadcasted_iota(jnp.int32, (GROUP, GROUP), 1)
    lower = (rows >= cols) & ((rows >= SPAN) == (cols >= SPAN))
    tri = lower.astype(F32)
    second = rows >= SPAN
    for g in range(MB):
        keep = 1.0 - split_ref[g]
        here = dec_ref[g * GROUP : (g + 1) * GROUP, :]
        here_t = dect_ref[:, g * GROUP : (g + 1) * GROUP]
        run = exact(tri, jnp.log(here[:, : 2 * H]))
        run_t = exact(jnp.log(here_t[: 2 * H, :]), tri, NT)
        for h in range(H):
            gap = run[:, h : h + 1] - run_t[h : h + 1, :]
            retain = jnp.exp(jnp.where(lower, gap, -1e30))
            gap = run[:, H + h : H + h + 1] - run_t[H + h : H + h + 1, :]
            moment = jnp.exp(jnp.where(lower, gap, -1e30))
            pairs = exact(retain, moment)
            theta = here_t[2 * H + h : 2 * H + h + 1, :]
            moment_run = jnp.exp(run_t[H + h : H + h + 1, :])
            carry = jnp.sum(retain * moment_run, axis=1, keepdims=True)
            last_weight = pairs[SPAN - 1 : SPAN, :] * theta * keep
            last_moment = moment[SPAN - 1 : SPAN, :] * theta * keep
            across = jnp.exp(run[:, h : h + 1]) * last_weight + carry * last_moment
            wf_ref[h, g] = pairs * theta + jnp.where(second, across, 0.0)
            lw_ref[h, g] = jnp.broadcast_to(last_weight, (8, GROUP))


def allowed_mask(split_ref):
    rows = lax.broadcasted_iota(jnp.int32, (ROWS, GROUP), 0)
    cols = lax.broadcasted_iota(jnp.int32, (ROWS, GROUP), 1)
    local = rows % GROUP
    group = rows // GROUP
    split = jnp.where(group == 0, split_ref[0], split_ref[1]) > 0.5
    return (local >= cols) & jnp.logical_not(split & (local >= SPAN) & (cols < SPAN))


def by_group(make):
    return jnp.concatenate([make(slice(0, GROUP), 0), make(slice(GROUP, ROWS), 1)], axis=0)


def attend(q, k, v, pk, pv, allowed):
    near = by_group(lambda s, g: dot(q[s], k[s], NT))
    far = dot(q, pk, NT) * SCALE
    near = jnp.where(allowed, near * SCALE, -1000000000.0)
    top = jnp.maximum(
        jnp.max(near, axis=-1, keepdims=True), jnp.max(far, axis=-1, keepdims=True)
    )
    near = jnp.exp(near - top)
    far = jnp.exp(far - top)
    inv = 1.0 / (jnp.sum(near, axis=-1, keepdims=True) + jnp.sum(far, axis=-1, keepdims=True))
    near = near * inv
    far = far * inv
    return near, far


def attend_out(near_half, far_half, v, pv):
    return by_group(lambda s, g: dot(near_half[s], v[s])) + dot(far_half, pv)


def unit(values):
    inv = lax.rsqrt(jnp.mean(values * values, axis=-1, keepdims=True) + EPS)
    return values * (inv * SCALE), inv


def unit_bwd(grad, values, inv):
    return (inv * SCALE) * (
        grad - values * (inv * inv * jnp.mean(values * grad, axis=-1, keepdims=True))
    )


def memory_terms(kn, qn, mv, wf_ref, lw_ref):
    second = lax.broadcasted_iota(jnp.int32, (GROUP, GROUP), 0) >= SPAN
    kept = []
    for g in range(MB):
        s = slice(g * GROUP, (g + 1) * GROUP)
        kh, qh = halves(kn[s]), halves(qn[s])
        wf = wf_ref[0, g]
        lw = jnp.where(second, lw_ref[0, g][0:1, :], 0.0)
        kk = dot3(kh, kh, NT) * lw
        qk = dot3(qh, kh, NT) * wf
        kk_half = halves(kk)
        mvh = halves(mv[s])
        err = mv[s] - dot3(kk_half, mvh)
        errh = halves(err)
        qk_half = halves(qk)
        kept.append((kh, qh, wf, lw, kk_half, qk_half, mvh, errh))
    return kept


def memory_out(kept):
    return jnp.concatenate([dot3(item[5], item[7]) for item in kept], axis=0)


def memory_bwd(kept, grad):
    grads_k, grads_q, grads_v = [], [], []
    for g in range(MB):
        kh, qh, wf, lw, kk_half, qk_half, mvh, errh = kept[g]
        gh = halves(grad[g * GROUP : (g + 1) * GROUP])
        d_qk = dot3(gh, errh, NT) * wf
        d_err = dot3(qk_half, gh, TN)
        deh = halves(d_err)
        d_v = d_err - dot3(kk_half, deh, TN)
        d_kk = dot3(deh, mvh, NT) * lw
        dqh = halves(d_qk)
        dkh = halves(d_kk)
        grads_q.append(dot3(dqh, kh))
        grads_k.append(dot3(dqh, qh, TN) - (dot3(dkh, kh) + dot3(dkh, kh, TN)))
        grads_v.append(d_v)
    return (
        jnp.concatenate(grads_k, axis=0),
        jnp.concatenate(grads_q, axis=0),
        jnp.concatenate(grads_v, axis=0),
    )


AXES = ("x", "z", "y")
MESH = pl.DeviceIdType.MESH


def position():
    me = lax.axis_index("fsdp")
    chip = me // 2
    return me % 2, (chip // 16, (chip // 4) % 4, chip % 4)


def device(core, spot):
    return (((spot[0] * 4 + spot[1]) * 4 + spot[2]) * 2 + core,)


def moved(spot, axis, by):
    return tuple((v + by + 4) % 4 if i == axis else v for i, v in enumerate(spot))


def cut(lanes, count):
    base, extra = divmod(lanes, count)
    runs, at = [], 0
    for i in range(count):
        size = base + (1 if i < extra else 0)
        runs.append((at * 128, size * 128))
        at += size
    return runs


def neighbours(core, spot):
    found = {}
    for axis in range(3):
        for by in (1, 2, 3):
            there = moved(spot, axis, by)
            found[axis, by] = (there, device(core, there))
    return found


class Sends:
    def __init__(self, send_sem, recv_sem):
        self.send_sem, self.recv_sem = send_sem, recv_sem
        self.slots, self.open = {}, []

    def copy(self, name, src, dst, target):
        slot = self.slots.setdefault(name, len(self.slots))
        return pltpu.make_async_remote_copy(
            src_ref=src, dst_ref=dst, send_sem=self.send_sem.at[slot], recv_sem=self.recv_sem.at[slot],
            device_id=target, device_id_type=MESH,
        )

    def start(self, name, make):
        self.copy(name, *make()).start()
        self.open.append((name, make))

    def arrived(self, name, ref, target):
        self.copy(name, ref, ref, target).wait_recv()

    def drain(self):
        for name, make in self.open:
            self.copy(name, *make()).wait_send()
        self.open = []


def greet(targets):
    barrier = pltpu.get_barrier_semaphore()
    for target in targets:
        pl.semaphore_signal(barrier, inc=1, device_id=target, device_id_type=MESH)
    pl.semaphore_wait(barrier, len(targets))


class Gather:
    def __init__(self, sends, outs, widths):
        self.sends, self.outs = sends, outs
        self.core, self.spot = position()
        self.other = 1 - self.core
        self.sibling = device(1 - self.core, self.spot)
        self.near = neighbours(self.core, self.spot)
        self.jobs = [
            [(i, part, cols) for part, cols in enumerate(cut(width // 128, 3))] for i, width in enumerate(widths)
        ]
        self.forwards = [[] for _ in widths]

    def peers(self):
        return [self.sibling] + [self.near[a, by][1] for a in range(3) for by in (1, 3)]

    def block(self, i, whole_axes, at, cols, half=None):
        index = [pl.ds(0, 4) if a in whole_axes else pl.ds(at[a], 1) for a in range(3)]
        half = self.core if half is None else half
        return self.outs[i].at[half, index[0], index[1], index[2], :, pl.ds(cols[0], cols[1])]

    def push(self, name, target, *where):
        def make():
            ref = self.block(*where)
            return ref, ref, target

        self.sends.start(name, make)

    def forward(self, name, *where):
        self.push(name, self.sibling, *where)
        self.forwards[where[0]].append((name, where))

    def plan(self, item, phase):
        for i, part, cols in self.jobs[item]:
            axis = (part + phase) % 3
            done = [(part + p) % 3 for p in range(phase)]
            sides = [self.near[axis, by] for by in (1, 3, 2)]
            halves_of = [(cols[0] + at, size) for at, size in cut(cols[1] // 128, 2)]
            yield i, part, cols, done, sides, halves_of

    def begin(self, item, phase):
        for i, part, cols, done, (right, left, _), two in self.plan(item, phase):
            for step, (a, b) in enumerate(((0, 1), (1, 0))):
                self.push((i, part, phase, "r", step), right[1], i, done, self.spot, two[a])
                self.push((i, part, phase, "l", step), left[1], i, done, self.spot, two[b])
            if phase == 2:
                self.forward((i, part, "f"), i, done, self.spot, cols)

    def relay(self, item, phase):
        for i, part, cols, done, (right, left, _), two in self.plan(item, phase):
            for side, source, target, cc in (("r", left, right, two[0]), ("l", right, left, two[1])):
                where = (i, done, source[0], cc)
                self.sends.arrived((i, part, phase, side, 0), self.block(*where), source[1])
                self.push((i, part, phase, side, 2), target[1], *where)
                if phase == 2:
                    self.forward((i, part, "f", side, 0), *where)

    def finish(self, item, phase):
        for i, part, cols, done, (right, left, far), two in self.plan(item, phase):
            for side, step, at, cc, source in (
                ("r", 1, left, two[1], left),
                ("l", 1, right, two[0], right),
                ("r", 2, far, two[0], left),
                ("l", 2, far, two[1], right),
            ):
                where = (i, done, at[0], cc)
                self.sends.arrived((i, part, phase, side, step), self.block(*where), source[1])
                if phase == 2:
                    self.forward((i, part, "f", side, step), *where)

    def received(self, item):
        for name, (i, done, at, cc) in self.forwards[item]:
            self.sends.arrived(name, self.block(i, done, at, cc, self.other), self.sibling)


W1 = 4 * HCOLS + 7 * AR
W2 = 4 * FB + D + 3 * 768
FSTEPS = H
JSTEPS = FFP // FB


def forward_kernel(
    split_ref, x_ref, d_ref, gain1_ref, gain2_ref, mask_ref, place_ref, dec_ref, dect_ref, pers_ref, mine0, mine1,
    a1_ref, a23_ref, proj_ref, h1_ref, lat_ref, wf_ref, lw_ref, back_ref, dz_ref, dmid_ref, grads_ref,
    inc0, inc1, stage0, stage1, w_buf, up_buf, down_buf, z_ref, wup_buf, wd_buf, wout_buf, small_buf,
    x2_ref, h2_ref, inv_ref, lat_out_ref, lat_up_ref, dl_down_ref, acc_ref, lat_acc_ref, dh_ref, dlat_ref,
    send_sem, recv_sem, local_sem, w_sem, j_sem,
):
    step = pl.program_id(0)
    mine, inc, stage, outs = (mine0, mine1), (inc0, inc1), (stage0, stage1), (a1_ref, a23_ref)
    sends = Sends(send_sem, recv_sem)
    ring = Gather(sends, outs, (W1, W2))
    core, spot = ring.core, ring.spot
    other = 1 - core

    def head_loads(h, slot):
        half, place = h // 4, pl.multiple_of((h % 4) * HCOLS, 128)
        return (
            pltpu.make_async_copy(
                a1_ref.at[half, :, :, :, :, pl.ds(place, HCOLS)], w_buf.at[slot], w_sem.at[slot, 0]
            ),
            pltpu.make_async_copy(
                a1_ref.at[1, h // 2, pl.ds(2 * (h % 2), 2), :, :, pl.ds(4 * HCOLS, HCOLS)],
                up_buf.at[slot],
                w_sem.at[slot, 1],
            ),
        )

    def down_load():
        return pltpu.make_async_copy(
            a1_ref.at[0, :, :, :, :, pl.ds(4 * HCOLS, HCOLS)], down_buf, local_sem.at[0]
        )

    def block_loads(j, slot):
        place = pl.multiple_of((j % 2) * 2 * FB, 128)
        return (
            pltpu.make_async_copy(
                a23_ref.at[j // 2, :, :, :, :, pl.ds(place, 2 * FB)], wup_buf.at[slot], j_sem.at[slot, 0]
            ),
            pltpu.make_async_copy(
                a23_ref.at[:, j, :, :, :, pl.ds(4 * FB + D, 3 * 768)], wd_buf.at[slot], j_sem.at[slot, 1]
            ),
        )

    def side_loads():
        return (
            pltpu.make_async_copy(a23_ref.at[1, :, :, :, :, pl.ds(4 * FB, D)], wout_buf, local_sem.at[0]),
            pltpu.make_async_copy(a23_ref.at[0, :, :, :, :, pl.ds(4 * FB, D)], small_buf, local_sem.at[1]),
        )

    @pl.when(step == 0)
    def _():
        greet(ring.peers())
        for i in range(2):
            sends.start(("pair", i), lambda i=i: (mine[i].at[other], inc[i], ring.sibling))
        own_copy = lambda i: pltpu.make_async_copy(
            stage[i], outs[i].at[core, spot[0], spot[1], spot[2]], local_sem.at[i]
        )
        for i in range(2):
            sends.arrived(("pair", i), inc[i], ring.sibling)
            own, theirs = mine[i][core], inc[i][...]
            first = jnp.where(core == 0, own, theirs)
            last = jnp.where(core == 0, theirs, own)
            stage[i][...] = jnp.concatenate([first, last], axis=0).astype(BF)
            own_copy(i).start()
        for i in range(2):
            own_copy(i).wait()
            ring.begin(i, 0)
        decay_kernel(split_ref, dec_ref, dect_ref, wf_ref, lw_ref)
        normed, _ = norm_fwd(x_ref[...].astype(F32), gain1_ref[...])
        h1_ref[...] = normed.astype(BF)
        ring.relay(0, 0)
        ring.relay(1, 0)
        ring.finish(0, 0)
        ring.begin(0, 1)
        ring.finish(1, 0)
        ring.relay(0, 1)
        ring.finish(0, 1)
        ring.begin(0, 2)
        ring.begin(1, 1)
        ring.relay(0, 2)
        ring.relay(1, 1)
        ring.finish(0, 2)
        ring.received(0)
        for copy in head_loads(0, 0):
            copy.start()
        down_load().start()
        ring.finish(1, 1)
        ring.begin(1, 2)
        down_load().wait()
        latent = dot(h1_ref[...], down_buf[...].reshape(D, HCOLS))
        mask = mask_ref[...]
        for part in range(7):
            s = slice(part * AR, (part + 1) * AR)
            lat_ref[:, s] = (latent[:, s] * mask).astype(BF)

    @pl.when(step == RELAY_STEP)
    def _():
        ring.relay(1, 2)

    @pl.when(step < FSTEPS)
    def _():
        slot = step % 2
        for copy in head_loads(step, slot):
            copy.wait()

        @pl.when(step + 1 < FSTEPS)
        def _():
            for copy in head_loads(step + 1, 1 - slot):
                copy.start()

        base = dot(h1_ref[...], w_buf[slot].reshape(D, HCOLS))
        up = up_buf[slot].reshape(HEAD, HCOLS)
        pieces = []
        for part in range(7):
            s = slice(part * AR, (part + 1) * AR)
            piece = base[:, part * HEAD : (part + 1) * HEAD] + dot(lat_ref[:, s], up[:, s], NT)
            proj_ref[:, part * HEAD : (part + 1) * HEAD] = piece
            pieces.append(piece)
        q, k, v = (pieces[i].astype(BF) for i in range(3))
        pk, pv = pers_ref[0, :, pl.ds(pl.multiple_of(step * HEAD, HEAD), HEAD)], pers_ref[
            1, :, pl.ds(pl.multiple_of(step * HEAD, HEAD), HEAD)
        ]
        near, far = attend(q, k, v, pk, pv, allowed_mask(split_ref))
        att = attend_out(near.astype(BF), far.astype(BF), v, pv)
        kn, _ = unit(pieces[3])
        qn, _ = unit(pieces[5])
        here = pl.ds(step, 1)
        mem = memory_out(memory_terms(kn, qn, pieces[4], wf_ref.at[here], lw_ref.at[here]))
        z_ref[:, pl.ds(pl.multiple_of(step * HEAD, HEAD), HEAD)] = (
            att + jax.nn.sigmoid(pieces[6]) * mem
        ).astype(BF)

    small = lambda lo, hi: small_buf[:, :, :, :, lo:hi].reshape(D, hi - lo)
    out_down = lambda: small(0, 128)
    out_up = lambda: small(128, 256)
    up_down = lambda: small(256, 512)
    down_up = lambda: small(512, 640)

    @pl.when(step == FSTEPS)
    def _():
        ring.finish(1, 2)
        ring.received(1)
        for copy in side_loads() + block_loads(0, 0):
            copy.start()
        for copy in side_loads():
            copy.wait()
        mask = mask_ref[...]
        z = z_ref[...]
        lat_out_ref[...] = (dot(z, out_down()) * mask).astype(BF)
        x2 = x_ref[...].astype(F32) + (
            dot(z, wout_buf[...].reshape(D, D)) + dot(lat_out_ref[...], out_up(), NT)
        )
        x2_ref[...] = x2
        normed, inv = norm_fwd(x2, gain2_ref[...])
        inv_ref[...] = jnp.broadcast_to(inv, inv_ref.shape)
        h2_ref[...] = normed.astype(BF)
        latent = dot(h2_ref[...], up_down())
        lat_up_ref[:, :AR] = (latent[:, :AR] * mask).astype(BF)
        lat_up_ref[:, AR:] = (latent[:, AR:] * mask).astype(BF)
        dl_down_ref[...] = (dot(d_ref[...], down_up()) * mask).astype(BF)
        acc_ref[...] = jnp.zeros_like(acc_ref)
        lat_acc_ref[...] = jnp.zeros_like(lat_acc_ref)
        dh_ref[...] = jnp.zeros_like(dh_ref)
        dlat_ref[...] = jnp.zeros_like(dlat_ref)

    @pl.when(step >= FSTEPS)
    def _():
        j = step - FSTEPS
        slot = j % 2
        for copy in block_loads(j, slot):
            copy.wait()

        @pl.when(j + 1 < JSTEPS)
        def _():
            for copy in block_loads(j + 1, 1 - slot):
                copy.start()

        h2 = h2_ref[...]
        d = d_ref[...]
        w_gate = wup_buf[slot, :, :, :, :, :FB].reshape(D, FB)
        w_lift = wup_buf[slot, :, :, :, :, FB:].reshape(D, FB)
        lat0, lat1 = lat_up_ref[:, :AR], lat_up_ref[:, AR:]

        def tall(half, lo, hi):
            return jnp.concatenate(
                [wd_buf[slot, half, :, :, :, k * 768 + lo : k * 768 + hi].reshape(256, hi - lo) for k in range(3)],
                axis=0,
            )

        wda, wdb = tall(0, 0, 768), tall(1, 0, 256)
        uu0, uu1, dd = tall(1, 256, 384), tall(1, 384, 512), tall(1, 512, 640)
        gate = dot(h2, w_gate) + dot(lat0, uu0, NT)
        lift = dot(h2, w_lift) + dot(lat1, uu1, NT)
        sig = jax.nn.sigmoid(gate)
        silu = gate * sig
        act = (silu * lift).astype(BF)
        acc_ref[:, :768] += dot(act, wda)
        acc_ref[:, 768:] += dot(act, wdb)
        lat_acc_ref[...] += dot(act, dd)
        d_act = dot(d[:, :768], wda, NT) + dot(d[:, 768:], wdb, NT) + dot(dl_down_ref[...], dd, NT)
        d_gate = (d_act * lift * (sig * (1.0 + gate * (1.0 - sig)))).astype(BF)
        d_lift = (d_act * silu).astype(BF)
        dh_ref[...] += dot(d_gate, w_gate, NT) + dot(d_lift, w_lift, NT)
        dlat_ref[:, :AR] += dot(d_gate, uu0)
        dlat_ref[:, AR:] += dot(d_lift, uu1)
        first = pl.multiple_of(j * 16, 16)
        for place, term in (
            (0, dot(d_gate, lat0, TN)),
            (1, dot(d_lift, lat1, TN)),
            (2, dot(act, dl_down_ref[...], TN)),
        ):
            shaped = term.reshape(3, 16, 16, AR).astype(BF)
            for k in range(3):
                if place < 2:
                    at = k * 256 + place * AR
                    grads_ref[0, pl.ds(first, 16), :, at : at + AR] = shaped[k]
                else:
                    grads_ref[1, pl.ds(first, 16), :, k * AR : (k + 1) * AR] = shaped[k]

    @pl.when(step == FSTEPS + JSTEPS - 1)
    def _():
        mask = mask_ref[...]
        lat_down = (lat_acc_ref[...] * mask).astype(BF)
        out = (x2_ref[...] + acc_ref[...] + dot(lat_down, down_up(), NT)).astype(BF)
        for m in range(MB):
            s = slice(m * GROUP, (m + 1) * GROUP)
            back_ref[:, m * D : (m + 1) * D] = dot(place_ref[m], out[s], TN).astype(BF)
        d = d_ref[...]
        h2 = h2_ref[...]
        z = z_ref[...]

        def put(half, at, value):
            grads_ref[half, :, :, at : at + AR] = value.reshape(64, 16, AR).astype(BF)

        put(0, 768, dot(d, lat_down, TN))
        dlu0 = (dlat_ref[:, :AR] * mask).astype(BF)
        dlu1 = (dlat_ref[:, AR:] * mask).astype(BF)
        put(1, 640, dot(h2, dlu0, TN))
        put(1, 768, dot(h2, dlu1, TN))
        ud = up_down()
        dh = dh_ref[...] + (dot(dlu0, ud[:, :AR], NT) + dot(dlu1, ud[:, AR:], NT))
        dmid = d.astype(F32) + norm_bwd(dh, x2_ref[...], inv_ref[:, :1], gain2_ref[...])
        dmid_ref[...] = dmid
        dmb = dmid.astype(BF)
        dlo = (dot(dmb, out_up()) * mask).astype(BF)
        put(1, 384, dot(z, dlo, TN))
        put(1, 512, dot(dmb, lat_out_ref[...], TN))
        dz_ref[...] = (dot(dmb, wout_buf[...].reshape(D, D), NT) + dot(dlo, out_down(), NT)).astype(BF)
        sends.drain()


RELAY_STEP = 3


def forward_call(split, x, d, gain1, gain2, mask, place, dec, dec_t, persistent, mine0, mine1):
    whole = lambda *shape: pl.BlockSpec(shape, lambda s: (0,) * len(shape))
    hbm = pl.BlockSpec(memory_space=pl.ANY)
    slots = 2 * (1 + 3 * (3 * 6 + 7))
    return pl.pallas_call(
        forward_kernel,
        grid=(FSTEPS + JSTEPS,),
        out_shape=(
            jax.ShapeDtypeStruct((2, 4, 4, 4, 16, W1), BF),
            jax.ShapeDtypeStruct((2, 4, 4, 4, 16, W2), BF),
            jax.ShapeDtypeStruct((ROWS, 7 * D), F32),
            jax.ShapeDtypeStruct((ROWS, D), BF),
            jax.ShapeDtypeStruct((ROWS, 7 * AR), BF),
            jax.ShapeDtypeStruct((H, MB, GROUP, GROUP), F32),
            jax.ShapeDtypeStruct((H, MB, 8, GROUP), F32),
            jax.ShapeDtypeStruct((GROUP, MB * D), BF),
            jax.ShapeDtypeStruct((ROWS, D), BF),
            jax.ShapeDtypeStruct((ROWS, D), F32),
            jax.ShapeDtypeStruct((2, 64, 16, 896), BF),
        ),
        in_specs=[
            pl.BlockSpec(memory_space=pltpu.SMEM),
            whole(ROWS, D),
            whole(ROWS, D),
            whole(1, D),
            whole(1, D),
            whole(ROWS, AR),
            whole(MB, GROUP, GROUP),
            whole(ROWS, 3 * H),
            whole(3 * H, ROWS),
            whole(2, NP, D),
            whole(2, 8, W1),
            whole(2, 8, W2),
        ],
        out_specs=(
            hbm,
            hbm,
            pl.BlockSpec((ROWS, HCOLS), lambda s: (0, jnp.minimum(s, FSTEPS - 1))),
            whole(ROWS, D),
            whole(ROWS, 7 * AR),
            whole(H, MB, GROUP, GROUP),
            whole(H, MB, 8, GROUP),
            whole(GROUP, MB * D),
            whole(ROWS, D),
            whole(ROWS, D),
            whole(2, 64, 16, 896),
        ),
        scratch_shapes=[
            pltpu.VMEM((8, W1), F32),
            pltpu.VMEM((8, W2), F32),
            pltpu.VMEM((16, W1), BF),
            pltpu.VMEM((16, W2), BF),
            pltpu.VMEM((2, 4, 4, 4, 16, HCOLS), BF),
            pltpu.VMEM((2, 2, 4, 16, HCOLS), BF),
            pltpu.VMEM((4, 4, 4, 16, HCOLS), BF),
            pltpu.VMEM((ROWS, D), BF),
            pltpu.VMEM((2, 4, 4, 4, 16, 2 * FB), BF),
            pltpu.VMEM((2, 2, 4, 4, 16, 3 * 768), BF),
            pltpu.VMEM((4, 4, 4, 16, D), BF),
            pltpu.VMEM((4, 4, 4, 16, D), BF),
            pltpu.VMEM((ROWS, D), F32),
            pltpu.VMEM((ROWS, D), BF),
            pltpu.VMEM((ROWS, 128), F32),
            pltpu.VMEM((ROWS, AR), BF),
            pltpu.VMEM((ROWS, 2 * AR), BF),
            pltpu.VMEM((ROWS, AR), BF),
            pltpu.VMEM((ROWS, D), F32),
            pltpu.VMEM((ROWS, AR), F32),
            pltpu.VMEM((ROWS, D), F32),
            pltpu.VMEM((ROWS, 2 * AR), F32),
            pltpu.SemaphoreType.DMA((slots,)),
            pltpu.SemaphoreType.DMA((slots,)),
            pltpu.SemaphoreType.DMA((2,)),
            pltpu.SemaphoreType.DMA((2, 2)),
            pltpu.SemaphoreType.DMA((2, 2)),
        ],
        compiler_params=pltpu.CompilerParams(
            collective_id=0, has_side_effects=True, vmem_limit_bytes=VMEM_LIMIT
        ),
        name="gather_forward",
    )(split, x, d, gain1, gain2, mask, place, dec, dec_t, persistent, mine0, mine1)


class Scatter:
    def __init__(self, sends, key, grads, out, inc0, total, inc1, inc2, inc3, t1, t2):
        self.sends, self.key, self.grads, self.out = sends, key, grads, out
        self.inc0, self.total, self.inc = inc0, total, (None, inc1, inc2, inc3)
        self.t1, self.t2 = t1, t2
        self.core, self.spot = position()
        self.other = 1 - self.core
        self.sibling = device(1 - self.core, self.spot)
        self.near = neighbours(self.core, self.spot)
        self.parts = [(part, pl.ds(*cols)) for part, cols in enumerate(cut(7, 3))]

    def peers(self):
        return [self.sibling] + [there[1] for there in self.near.values()]

    def pair(self):
        for x in range(4):
            self.sends.start(
                (self.key, "pair", x),
                lambda x=x: (
                    self.grads.at[self.other, pl.ds(16 * x, 16)],
                    self.inc0.at[x],
                    self.sibling,
                ),
            )

    def source(self, phase, part, at):
        axis = (part + phase - 1) % 3
        cs = self.parts[part][1]
        if phase == 1:
            index = tuple(at if a == axis else slice(None) for a in range(3))
            return self.total, index + (slice(None), cs)
        rest = [a for a in range(3) if a != part]
        if phase == 2:
            index = (at, slice(None)) if rest[0] == axis else (slice(None), at)
            return self.t1, index + (slice(None), cs)
        return self.t2, (at, slice(None), cs)

    def landing(self, phase, part, k):
        return (k,) + (slice(None),) * (4 - phase) + (self.parts[part][1],)

    def send(self, phase):
        for part, _ in self.parts:
            axis = (part + phase - 1) % 3
            for k, by in enumerate((2, 1, 3)):
                to = self.near[axis, by]

                def make(part=part, axis=axis, to=to, k=k):
                    ref, index = self.source(phase, part, to[0][axis])
                    return ref.at[index], self.inc[phase].at[self.landing(phase, part, k)], to[1]

                self.sends.start((self.key, part, phase, by), make)

    def add(self, phase):
        for part, cs in self.parts:
            axis = (part + phase - 1) % 3
            ref, index = self.source(phase, part, self.spot[axis])
            acc = ref[index].astype(F32)
            for k, by in enumerate((2, 1, 3)):
                here = self.landing(phase, part, k)
                source = self.near[axis, 4 - by][1]
                self.sends.arrived((self.key, part, phase, by), self.inc[phase].at[here], source)
                acc = acc + self.inc[phase][here].astype(F32)
            if phase == 1:
                self.t1[:, :, :, cs] = acc.astype(BF)
            elif phase == 2:
                self.t2[:, :, cs] = acc.astype(BF)
            else:
                self.out[self.core, :, cs] = acc

    def add_pair(self):
        for x in range(4):
            self.sends.arrived((self.key, "pair", x), self.inc0.at[x], self.sibling)
            both = self.grads[self.core, pl.ds(16 * x, 16)].astype(F32) + self.inc0[x].astype(F32)
            self.total[x] = both.reshape(4, 4, 16, 896).astype(BF)

    def swap(self):
        self.sends.start(
            (self.key, "last"), lambda: (self.out.at[self.core], self.out.at[self.core], self.sibling)
        )

    def swapped(self):
        self.sends.arrived((self.key, "last"), self.out.at[self.other], self.sibling)


def backward_kernel(
    split_ref, x_ref, gain_ref, mask_ref, place_ref, proj_ref, dz_ref, dmid_ref, h1_ref, lat_ref,
    w_ref, down_ref, up_ref, pers_ref, wf_ref, lw_ref, ffn_ref,
    back_ref, ffn_out, heads_out,
    dh_ref, dlat_ref, grads_ref, *rest,
):
    step = pl.program_id(0)
    send_sem, recv_sem = rest[-2:]
    sends = Sends(send_sem, recv_sem)
    first_sums = Scatter(sends, 0, ffn_ref, *rest[:8])
    last_sums = Scatter(sends, 1, grads_ref, *rest[8:16])

    @pl.when(step == 0)
    def _():
        greet(first_sums.peers())
        first_sums.pair()
        dh_ref[...] = jnp.zeros_like(dh_ref)
        dlat_ref[...] = jnp.zeros_like(dlat_ref)

    @pl.when(step == 2)
    def _():
        first_sums.add_pair()
        first_sums.send(1)

    @pl.when(step == 5)
    def _():
        first_sums.add(1)
        first_sums.send(2)

    @pl.when(step == 6)
    def _():
        first_sums.add(2)
        first_sums.send(3)

    @pl.when(step == 7)
    def _():
        first_sums.add(3)
        first_sums.swap()

    pieces = [proj_ref[:, p * HEAD : (p + 1) * HEAD] for p in range(7)]
    q, k, v = (pieces[i].astype(BF) for i in range(3))
    pk, pv = pers_ref[0], pers_ref[1]
    near, far = attend(q, k, v, pk, pv, allowed_mask(split_ref))
    near_half = near.astype(BF)
    dz = dz_ref[...]
    d_near = by_group(lambda s, g: dot(dz[s], v[s], NT))
    d_far = dot(dz, pv, NT)
    d_v = by_group(lambda s, g: dot(near_half[s], dz[s], TN))
    total = jnp.sum(d_near * near, axis=-1, keepdims=True) + jnp.sum(
        d_far * far, axis=-1, keepdims=True
    )
    ds_near = (near * (d_near - total) * SCALE).astype(BF)
    ds_far = (far * (d_far - total) * SCALE).astype(BF)
    d_q = by_group(lambda s, g: dot(ds_near[s], k[s])) + dot(ds_far, pk)
    d_k = by_group(lambda s, g: dot(ds_near[s], q[s], TN))

    dzf = dz.astype(F32)
    opening = jax.nn.sigmoid(pieces[6])
    kn, k_inv = unit(pieces[3])
    qn, q_inv = unit(pieces[5])
    kept = memory_terms(kn, qn, pieces[4], wf_ref, lw_ref)
    mem = memory_out(kept)
    d_open = dzf * mem * (opening * (1.0 - opening))
    d_kn, d_qn, d_mv = memory_bwd(kept, dzf * opening)
    d_mk = unit_bwd(d_kn, pieces[3], k_inv)
    d_mq = unit_bwd(d_qn, pieces[5], q_inv)
    dy = [item.astype(BF) for item in (d_q, d_k, d_v, d_mk, d_mv, d_mq, d_open)]
    dh_ref[...] += dot(jnp.concatenate(dy, axis=1), w_ref[0], NT)
    first = pl.multiple_of(step * 8, 8)
    for part in range(7):
        s = slice(part * AR, (part + 1) * AR)
        dlat_ref[:, s] += dot(dy[part], up_ref[0, :, s])
        grads_ref[1, pl.ds(first, 8), :, s] = (
            dot(dy[part], lat_ref[:, s], TN).reshape(8, 16, AR).astype(BF)
        )

    @pl.when(step == pl.num_programs(0) - 1)
    def _():
        mask = mask_ref[...]
        dlat = jnp.concatenate(
            [(dlat_ref[:, p * AR : (p + 1) * AR] * mask).astype(BF) for p in range(7)], axis=1
        )
        grads_ref[0] = dot(h1_ref[...], dlat, TN).reshape(64, 16, 7 * AR).astype(BF)
        last_sums.pair()
        dh = dh_ref[...] + dot(dlat, down_ref[0], NT)
        x = x_ref[...].astype(F32)
        inv = lax.rsqrt(jnp.mean(x * x, axis=-1, keepdims=True) + EPS)
        dx = (dmid_ref[...] + norm_bwd(dh, x, inv, gain_ref[...])).astype(BF)
        for m in range(MB):
            s = slice(m * GROUP, (m + 1) * GROUP)
            back_ref[:, m * D : (m + 1) * D] = dot(place_ref[m], dx[s], TN).astype(BF)
        last_sums.add_pair()
        last_sums.send(1)
        first_sums.swapped()
        last_sums.add(1)
        last_sums.send(2)
        last_sums.add(2)
        last_sums.send(3)
        last_sums.add(3)
        last_sums.swap()
        last_sums.swapped()
        ffn_out[...] = first_sums.out[...]
        heads_out[...] = last_sums.out[...]
        sends.drain()


def backward_call(split, x, gain, mask, place, proj, dz, dmid, h1, lat, a1, persistent, wf, lw, grads_ffn):
    whole = lambda *shape: pl.BlockSpec(shape, lambda h: (0,) * len(shape))
    buffers = [
        pltpu.VMEM((2, 16, 896), F32),
        pltpu.VMEM((4, 16, 16, 896), BF),
        pltpu.VMEM((4, 4, 4, 16, 896), BF),
        pltpu.VMEM((3, 4, 4, 16, 896), BF),
        pltpu.VMEM((3, 4, 16, 896), BF),
        pltpu.VMEM((3, 16, 896), BF),
        pltpu.VMEM((4, 4, 16, 896), BF),
        pltpu.VMEM((4, 16, 896), BF),
    ]
    slots = 2 * (4 + 3 * 9 + 1)
    return pl.pallas_call(
        backward_kernel,
        grid=(H,),
        out_shape=(
            jax.ShapeDtypeStruct((GROUP, MB * D), BF),
            jax.ShapeDtypeStruct((2, 16, 896), F32),
            jax.ShapeDtypeStruct((2, 16, 896), F32),
        ),
        in_specs=[
            pl.BlockSpec(memory_space=pltpu.SMEM),
            whole(ROWS, D),
            whole(1, D),
            whole(ROWS, AR),
            whole(MB, GROUP, GROUP),
            pl.BlockSpec((ROWS, HCOLS), lambda h: (0, h)),
            pl.BlockSpec((ROWS, HEAD), lambda h: (0, h)),
            whole(ROWS, D),
            whole(ROWS, D),
            whole(ROWS, 7 * AR),
            pl.BlockSpec((1, D, HCOLS), lambda h: (h // 4, 0, h % 4)),
            pl.BlockSpec((1, D, HCOLS), lambda h: (0, 0, 4)),
            pl.BlockSpec((1, HEAD, HCOLS), lambda h: (1, h, 4)),
            pl.BlockSpec((2, NP, HEAD), lambda h: (0, 0, h)),
            pl.BlockSpec((1, MB, GROUP, GROUP), lambda h: (h, 0, 0, 0)),
            pl.BlockSpec((1, MB, 8, GROUP), lambda h: (h, 0, 0, 0)),
            pl.BlockSpec(memory_space=pltpu.VMEM),
        ],
        out_specs=(
            whole(GROUP, MB * D),
            pl.BlockSpec(memory_space=pltpu.VMEM),
            pl.BlockSpec(memory_space=pltpu.VMEM),
        ),
        scratch_shapes=[
            pltpu.VMEM((ROWS, D), F32),
            pltpu.VMEM((ROWS, 7 * AR), F32),
            pltpu.VMEM((2, 64, 16, 896), BF),
        ]
        + buffers * 2
        + [pltpu.SemaphoreType.DMA((slots,)), pltpu.SemaphoreType.DMA((slots,))],
        compiler_params=pltpu.CompilerParams(
            collective_id=1, has_side_effects=True, vmem_limit_bytes=VMEM_LIMIT
        ),
        name="backward_scatter",
    )(split, x, gain, mask, place, proj, dz, dmid, h1, lat, a1, a1, a1, persistent, wf, lw, grads_ffn)


def by_rank(value, parts):
    rows = value.shape[1]
    return value.reshape(NAD, rows, parts, R).transpose(1, 2, 0, 3).reshape(rows, parts * AR)


def by_rank_t(value, parts):
    cols = value.shape[2]
    return value.reshape(NAD, parts, R, cols).transpose(3, 1, 0, 2).reshape(cols, parts * AR)


def pack_shards(w_in, w_out, w_up, w_down, in_down, in_up, out_down, out_up, up_down, up_up, down_down, down_up):
    rows = w_in.shape[0]
    heads = w_in.reshape(rows, 7, H, HEAD).transpose(0, 2, 1, 3).reshape(rows, 2, 4 * HCOLS)
    first = jnp.stack(
        [
            jnp.concatenate([heads[:, 0], by_rank(in_down, 7)], axis=1),
            jnp.concatenate([heads[:, 1], by_rank_t(in_up, 7)], axis=1),
        ]
    )
    up = w_up.reshape(rows, 2, N_DEV, FF_SHARD)
    up = jnp.pad(up, ((0, 0), (0, 0), (0, 0), (0, FF_PAD - FF_SHARD)))
    up = up.reshape(rows, 2, 4, 32, 3, 8).transpose(0, 2, 1, 4, 3, 5).reshape(rows, 2, 4 * FB)
    small = jnp.concatenate(
        [by_rank(out_down, 1), by_rank_t(out_up, 1), by_rank(up_down, 2), by_rank_t(down_up, 1)], axis=1
    )
    small = jnp.pad(small, ((0, 0), (0, D - small.shape[1])))
    rest = jnp.concatenate([w_down[:, 768:], by_rank_t(up_up, 2), by_rank(down_down, 1)], axis=1)
    rest = jnp.pad(rest, ((0, 0), (0, 128)))
    tall = jnp.pad(jnp.stack([w_down[:, :768], rest]), ((0, 0), (0, FF_PAD - FF_SHARD), (0, 0)))
    tall = tall.reshape(2, 3, 8, 768).transpose(0, 2, 1, 3).reshape(2, 8, 3 * 768)
    second = jnp.stack(
        [
            jnp.concatenate([up[:, 0], small, tall[0]], axis=1),
            jnp.concatenate([up[:, 1], w_out, tall[1]], axis=1),
        ]
    )
    return first, second


def un_rank(value, parts):
    rows = value.shape[0]
    return value.reshape(rows, parts, NAD, R).transpose(2, 0, 1, 3).reshape(NAD, rows, parts * R)


def un_rank_t(value, parts):
    cols = value.shape[0]
    return value.reshape(cols, parts, NAD, R).transpose(2, 1, 3, 0).reshape(NAD, parts * R, cols)


def unpack_grads(ffn_chip, heads_chip, core):
    def rows8(value):
        return lax.dynamic_slice_in_dim(value, core * 8, 8, axis=0)

    grad_id = un_rank(rows8(heads_chip[0]), 7)
    grad_iu = un_rank_t(rows8(heads_chip[1]), 7)

    def rows22(value, width):
        value = rows8(value).reshape(8, 3, width).transpose(1, 0, 2)
        return value.reshape(FF_PAD, width)[:FF_SHARD]

    grad_uu = un_rank_t(rows22(ffn_chip[0, :, :768], 256), 2)
    grad_dd = un_rank(rows22(ffn_chip[1, :, :384], AR), 1)
    grad_du = un_rank_t(rows8(ffn_chip[0, :, 768:]), 1)
    grad_od = un_rank(rows8(ffn_chip[1, :, 384:512]), 1)
    grad_ou = un_rank_t(rows8(ffn_chip[1, :, 512:640]), 1)
    grad_ud = un_rank(rows8(ffn_chip[1, :, 640:896]), 2)
    return grad_id, grad_iu, grad_od, grad_ou, grad_ud, grad_uu, grad_dd, grad_du


def body(
    tokens, cotangent, decays, route, lengths, adapter_ids, gain_mix, gain_ffn, persistent,
    w_in, w_out, w_up, w_down, in_down, in_up, out_down, out_up, up_down, up_up, down_down, down_up,
):
    me = lax.axis_index("fsdp")
    packed = pack_shards(
        w_in, w_out, w_up, w_down, in_down, in_up, out_down, out_up, up_down, up_up, down_down, down_up
    )
    first, second = (item.astype(F32) for item in packed)

    spots = jnp.arange(GROUP, dtype=jnp.int32)
    own = lax.dynamic_slice_in_dim(route, me * GROUP, GROUP, axis=1)
    send = (own[:, None, :] // GROUP == spots[None, :, None]).astype(BF)
    blocks = route.reshape(MB, N_DEV, GROUP)
    landing = jnp.sum(jnp.where(blocks // GROUP == me, blocks % GROUP, 0), axis=2)
    place = (landing[:, None, :] == spots[None, :, None]).astype(BF)

    def permute(onehot, values):
        return jnp.einsum("mij,mjd->mid", onehot, values, preferred_element_type=F32).astype(BF)

    def exchange(values):
        return lax.all_to_all(values, "fsdp", split_axis=0, concat_axis=0, tiled=True)

    out_x = permute(send, tokens)
    out_d = permute(send, cotangent)
    out_r = permute(send, decays)
    sent = jnp.concatenate(
        [out_x[0], out_x[1], out_d[0], out_d[1], out_r[0], out_r[1], jnp.zeros((GROUP, 80), BF)], axis=1
    )
    got = exchange(sent)
    at = lambda lo, width: jnp.stack([got[:, lo : lo + width], got[:, lo + width : lo + 2 * width]])
    x = permute(place, at(0, D)).reshape(ROWS, D)
    d = permute(place, at(2 * D, D)).reshape(ROWS, D)
    dec = permute(place, at(4 * D, 3 * H)).astype(F32).reshape(ROWS, 3 * H)
    lengths, ids = lengths[:, 0], adapter_ids[:, 0]
    split = (lengths[:, 0] < GROUP).astype(F32)
    row_ids = jnp.where(spots[None, :] >= lengths[:, :1], ids[:, 1:], ids[:, :1]).reshape(ROWS)
    mask = (row_ids[:, None] == (jnp.arange(AR) // R)[None, :]).astype(F32)
    gain_mix, gain_ffn = gain_mix[None, :], gain_ffn[None, :]
    a1, _, proj, h1, lat, wf, lw, back, dz, dmid, grads_ffn = forward_call(
        split, x, d, gain_mix, gain_ffn, mask, place, dec, dec.T, persistent, first, second
    )
    back_grad, ffn_chip, heads_chip = backward_call(
        split, x, gain_mix, mask, place, proj, dz, dmid, h1, lat, a1.reshape(2, D, W1), persistent, wf, lw, grads_ffn
    )

    def home(values):
        values = exchange(values)
        return jnp.einsum(
            "mij,mid->mjd", send, values.reshape(GROUP, MB, D).transpose(1, 0, 2), preferred_element_type=F32
        ).astype(BF)

    return (home(back), home(back_grad)) + unpack_grads(ffn_chip, heads_chip, me % 2)


def solution(mesh):
    rows, cols = P(None, "fsdp", None), P(None, None, "fsdp")
    weight = P("fsdp", None)
    return jax.shard_map(
        body,
        mesh=mesh,
        in_specs=(rows, rows, rows, P(), rows, rows, P(), P(), P())
        + (weight,) * 4
        + (rows, cols) * 4,
        out_specs=(rows, rows) + (rows, cols) * 4,
        check_vma=False,
    )
```

time: 320 us -> 293 us (0.916)
  Pallas kernels: 239 us -> 201 us
  waiting for transfers between devices: 14.7 us -> 26.4 us
    pallas_call x6 -> x2, Pallas kernels: 239 us -> 201 us  [the longest x1 138 us: forward_call(): pl.pallas_call(forward_kernel, grid=(FSTEPS + JSTEPS,), out_shape=(jax.Sh...]
    all_to_all x3, waiting for transfers between devices: 14.7 us -> 26.4 us  [exchange(): lax.all_to_all(values, 'fsdp', split_axis=0, concat_axis=0, tiled=True)]
    unnamed x53 -> x58, local copies, waits for them, and re-layouts: 10.1 us -> 10.1 us
  transfers between devices with their start and end apart: 3 -> 3, of which waited for: 2 -> 3; matrix products, arithmetic and copies ran while one was open for 7% -> 7% of each run, Pallas kernels for 35% -> 0%
where the time goes in v2:
time: 293 us; the launch traced here: 292 us
  Pallas kernels  201 us (69%)
  local copies, waits for them, and re-layouts  27.6 us (9%)
  waiting for transfers between devices  26.4 us (9%)
  starting transfers between devices  21.4 us (7%)
  other arithmetic  8 us (3%)
  matrix products  6.43 us (2%)
    pallas_call x1, Pallas kernels, forward_call(): pl.pallas_call(forward_kernel, grid=(FSTEPS + JSTEPS,), out_shape=(jax.Sh...  138 us
    pallas_call x1, Pallas kernels, backward_call(): pl.pallas_call(backward_kernel, grid=(H,), out_shape=(jax.ShapeDtypeStruc...  62.6 us
    all_to_all x3, waiting for transfers between devices, exchange(): lax.all_to_all(values, 'fsdp', split_axis=0, concat_axis=0, tiled=True)  26.4 us
    all_to_all x3, starting transfers between devices, exchange(): lax.all_to_all(values, 'fsdp', split_axis=0, concat_axis=0, tiled=True)  21.4 us
    unnamed x58, local copies, waits for them, and re-layouts  10.1 us
  transfers between devices with their start and end apart: 3, of which 3 were waited for; matrix products, arithmetic and copies ran while one was open for 7% of the time, Pallas kernels for 0%

profile of v2, /device:TPU:1, one launch (start us, length us, event | category | flops | bytes accessed | tf_op | source)
XLA Modules:
  0.0 292.0 jit_solution(13100265117329295274)
XLA Ops:
  1.4 1.0 convolution_convert_fusion.6
  3.4 1.1 concatenate.21
  5.0 1.4 reduce.6
  6.4 1.6 reshape.317
  8.1 11.5 %all-to-all-start = ((bf16[128,2,2112]{2,1,0:T(2,128)(2,1)}), bf16[128,2,2112]{2,1,0:T(2,128)(2,1)S(1)}, u32[]{:S(2)}, u32[]{:S(2)}) async-start(bf16[128,2,2112]{2,1,0:T(2,128)(2,1)} %reshape.317), calls=%async_computation | async-start | bytes 2228224 | tf_op jit(solution)/shard_map/all_to_all | solution.py:1012
  23.5 1.3 reshape.270
  26.1 1.7 reshape.272
  30.5 8.9 %all-to-all-done = bf16[128,2,2112]{2,1,0:T(2,128)(2,1)S(1)} async-done(((bf16[128,2,2112]{2,1,0:T(2,128)(2,1)}), bf16[128,2,2112]{2,1,0:T(2,128)(2,1)S(1)}, u32[]{:S(2)}, u32[]{:S(2)}) %all-to-all-start) | async-done | bytes 1081376 | tf_op jit(solution)/shard_map/all_to_all | solution.py:1012
  39.4 1.2 reshape.318
  42.1 1.1 convolution_convert_fusion.2
  43.1 1.1 convolution_convert_fusion.3
  44.2 138.1 %gather_forward.1 = (bf16[2,4,4,4,16,4480]{5,4,3,2,1,0:T(8,128)(2,1)}, bf16[2,4,4,4,16,6400]{5,4,3,2,1,0:T(8,128)(2,1)}, f32[256,7168]{1,0:T(8,128)}, bf16[256,1...) custom-call(f32[2]{0:T(128)} %compare_convert_fusion.1.split_ref, ...), custom_call_target="tpu_custom_call" | custom-call | tf_op jit(solution)/shard_map/gather_forward/pallas_call | solution.py:594
  182.4 62.6 %backward_scatter.1 = (bf16[128,2048]{1,0:T(8,128)(2,1)}, f32[2,16,896]{2,1,0:T(8,128)}, f32[2,16,896]{2,1,0:T(8,128)}) custom-call(f32[2]{0:T(128)} %compare_convert_fusion.1.split_ref, bf16[256,1024]{1,0:T(8,128)(2,1)} %bitcast.196, f32[1,1024]{1,0:T(1,128)} %bitcast.230, f32[256,128]{1,0:T(8,128)} %compare_convert_fusion.mask_ref, ...), custom_call_target="tpu_custom_call" | custom-call | tf_op jit(solution)/shard_map/backward_scatter/pallas_call | solution.py:876
  247.1 0.9 slice.130
  248.0 1.0 reduce.7
  249.0 1.2 reshape.319
  250.2 1.0 reduce.8
  251.2 1.2 reshape.321
  252.4 5.2 %all-to-all-start.2 = ((bf16[128,2,1024]{2,1,0:T(2,128)(2,1)}), bf16[128,2,1024]{2,1,0:T(2,128)(2,1)S(1)}, u32[]{:S(2)}, u32[]{:S(2)}) async-start(bf16[128,2,1024]{2,1,0:T(2,128)(2,1)} %reshape.321), calls=%async_computation.2 | async-start | bytes 1048576 | tf_op jit(solution)/shard_map/all_to_all | solution.py:1012
  257.7 13.4 %all-to-all-done.2 = bf16[128,2,1024]{2,1,0:T(2,128)(2,1)S(1)} async-done(((bf16[128,2,1024]{2,1,0:T(2,128)(2,1)}), bf16[128,2,1024]{2,1,0:T(2,128)(2,1)S(1)}, u32[]{:S(2)}, u32[]{:S(2)}) %all-to-all-start.2) | async-done | bytes 524320 | tf_op jit(solution)/shard_map/all_to_all | solution.py:1012
  271.1 4.8 %all-to-all-start.1 = ((bf16[128,2,1024]{2,1,0:T(2,128)(2,1)}), bf16[128,2,1024]{2,1,0:T(2,128)(2,1)S(1)}, u32[]{:S(2)}, u32[]{:S(2)}) async-start(bf16[128,2,1024]{2,1,0:T(2,128)(2,1)} %reshape.319), calls=%async_computation.1 | async-start | bytes 1048576 | tf_op jit(solution)/shard_map/all_to_all | solution.py:1012
  284.1 1.1 convolution_convert_fusion
  285.2 4.1 %all-to-all-done.1 = bf16[128,2,1024]{2,1,0:T(2,128)(2,1)S(1)} async-done(((bf16[128,2,1024]{2,1,0:T(2,128)(2,1)}), bf16[128,2,1024]{2,1,0:T(2,128)(2,1)S(1)}, u32[]{:S(2)}, u32[]{:S(2)}) %all-to-all-start.1) | async-done | bytes 524320 | tf_op jit(solution)/shard_map/all_to_all | solution.py:1012
  290.9 1.1 convolution_convert_fusion.1
  (145 shorter events, 23.2 us)
Async XLA Ops:
  0.6 1.8 copy-start
  0.7 2.2 copy-start.2
  8.0 11.6 %copy-start.6 = (s32[2,16384]{1,0:T(2,128)S(1)}, s32[2,16384]{1,0:T(2,128)}, u32[]{:S(2)}) copy-start(s32[2,16384]{1,0:T(2,128)} %param.24) | copy-start | bytes 393220
  8.0 11.8 %copy-start.20 = (s32[2,1,2]{2,1,0:T(1,128)S(1)}, s32[2,1,2]{2,1,0:T(1,128)}, u32[]{:S(2)}) copy-start(s32[2,1,2]{2,1,0:T(1,128)} %param.26) | copy-start | bytes 52
  8.0 11.8 %copy-start.21 = (s32[2,1,2]{2,1,0:T(1,128)S(1)}, s32[2,1,2]{2,1,0:T(1,128)}, u32[]{:S(2)}) copy-start(s32[2,1,2]{2,1,0:T(1,128)} %param.25) | copy-start | bytes 52
  8.0 12.6 %copy-start.12 = (bf16[8,22,16]{1,2,0:T(8,128)(2,1)S(1)}, bf16[8,22,16]{1,2,0:T(8,128)(2,1)}, u32[]{:S(2)}) copy-start(bf16[8,22,16]{1,2,0:T(8,128)(2,1)} %param.40) | copy-start | bytes 16900
  8.0 12.6 %copy-start.17 = (bf16[8,8,16]{2,1,0:T(8,128)(2,1)S(1)}, bf16[8,8,16]{2,1,0:T(8,128)(2,1)}, u32[]{:S(2)}) copy-start(bf16[8,8,16]{2,1,0:T(8,128)(2,1)} %param.36) | copy-start | bytes 6148
  8.0 12.7 %copy-start.18 = (bf16[8,16,8]{1,2,0:T(8,128)(2,1)S(1)}, bf16[8,16,8]{1,2,0:T(8,128)(2,1)}, u32[]{:S(2)}) copy-start(bf16[8,16,8]{1,2,0:T(8,128)(2,1)} %param.37) | copy-start | bytes 6148
  8.1 12.8 %copy-start.19 = (bf16[8,16,8]{1,2,0:T(8,128)(2,1)S(1)}, bf16[8,16,8]{1,2,0:T(8,128)(2,1)}, u32[]{:S(2)}) copy-start(bf16[8,16,8]{1,2,0:T(8,128)(2,1)} %param.41) | copy-start | bytes 6148
  8.1 12.9 %copy-start.13 = (bf16[8,8,32]{2,1,0:T(8,128)(2,1)S(1)}, bf16[8,8,32]{2,1,0:T(8,128)(2,1)}, u32[]{:S(2)}) copy-start(bf16[8,8,32]{2,1,0:T(8,128)(2,1)} %param.38) | copy-start | bytes 12292
  8.1 13.8 %copy-start.11 = (bf16[8,32,22]{1,0,2:T(8,128)(2,1)S(1)}, bf16[8,32,22]{1,0,2:T(8,128)(2,1)}, u32[]{:S(2)}) copy-start(bf16[8,32,22]{1,0,2:T(8,128)(2,1)} %param.39) | copy-start | bytes 33796
  8.1 14.3 %copy-start.10 = (bf16[22,1024]{1,0:T(8,128)(2,1)S(1)}, bf16[22,1024]{1,0:T(8,128)(2,1)}, u32[]{:S(2)}) copy-start(bf16[22,1024]{1,0:T(8,128)(2,1)} %param.33) | copy-start | bytes 135172
  8.1 14.3 %slice-start = ((bf16[22,1024]{1,0:T(8,128)(2,1)}), bf16[22,256]{1,0:T(8,128)(2,1)S(1)}, s32[]{:S(2)}) async-start(bf16[22,1024]{1,0:T(8,128)(2,1)} %param.33), calls=%async_computation.3 | async-start | bytes 24576 | tf_op jit(solution)/shard_map/slice | solution.py:948
  8.1 31.3 %all-to-all-start = ((bf16[128,2,2112]{2,1,0:T(2,128)(2,1)}), bf16[128,2,2112]{2,1,0:T(2,128)(2,1)S(1)}, u32[]{:S(2)}, u32[]{:S(2)}) async-start(bf16[128,2,2112]{2,1,0:T(2,128)(2,1)} %reshape.317), calls=%async_computation | async-start | bytes 2228224 | tf_op jit(solution)/shard_map/all_to_all | solution.py:1012
  19.6 2.8 copy-start.8
  19.9 2.9 %copy-start.14 = (bf16[8,8,112]{2,1,0:T(8,128)(2,1)S(1)}, bf16[8,8,112]{2,1,0:T(8,128)(2,1)}, u32[]{:S(2)}) copy-start(bf16[8,8,112]{2,1,0:T(8,128)(2,1)} %param.34) | copy-start | bytes 43012
  22.0 1.1 copy-start.15
  41.3 3.0 %copy-start.5 = (f32[2,3,8,128]{3,2,0,1:T(8,128)}, f32[2,3,8,128]{3,2,0,1:T(8,128)S(1)}, u32[]{:S(2)}) copy-start(f32[2,3,8,128]{3,2,0,1:T(8,128)S(1)} %copy.218) | copy-start | bytes 73732
  182.4 65.7 %copy-start.3 = (bf16[128,2048]{1,0:T(8,128)(2,1)S(1)}, bf16[128,2048]{1,0:T(8,128)(2,1)}, u32[]{:S(2)}) copy-start(bf16[128,2048]{1,0:T(8,128)(2,1)} %get-tuple-element.23) | copy-start | bytes 1572868
  247.1 3.0 %copy-start.4 = (bf16[128,2048]{1,0:T(8,128)(2,1)S(1)}, bf16[128,2048]{1,0:T(8,128)(2,1)}, u32[]{:S(2)}) copy-start(bf16[128,2048]{1,0:T(8,128)(2,1)} %get-tuple-element.33) | copy-start | bytes 1572868
  251.2 6.5 %copy-start.7 = (f32[2,16,896]{2,1,0:T(8,128)S(1)}, f32[2,16,896]{2,1,0:T(8,128)}, u32[]{:S(2)}) copy-start(f32[2,16,896]{2,1,0:T(8,128)} %get-tuple-element.34) | copy-start | bytes 344068
  252.4 18.7 %all-to-all-start.2 = ((bf16[128,2,1024]{2,1,0:T(2,128)(2,1)}), bf16[128,2,1024]{2,1,0:T(2,128)(2,1)S(1)}, u32[]{:S(2)}, u32[]{:S(2)}) async-start(bf16[128,2,1024]{2,1,0:T(2,128)(2,1)} %reshape.321), calls=%async_computation.2 | async-start | bytes 1048576 | tf_op jit(solution)/shard_map/all_to_all | solution.py:1012
  271.1 18.3 %all-to-all-start.1 = ((bf16[128,2,1024]{2,1,0:T(2,128)(2,1)}), bf16[128,2,1024]{2,1,0:T(2,128)(2,1)S(1)}, u32[]{:S(2)}, u32[]{:S(2)}) async-start(bf16[128,2,1024]{2,1,0:T(2,128)(2,1)} %reshape.319), calls=%async_computation.1 | async-start | bytes 1048576 | tf_op jit(solution)/shard_map/all_to_all | solution.py:1012
  289.8 2.2 copy-start.1
  (2 other events, 2.2 us)
